TPU v7x, 768 devices: a whole 4x8x12 slice. The times are simulated.
768 devices in a mesh: gx: 96 (over x, z, core), gy: 8 (over y).
Axes of the slice: x: 4, y: 8, z: 12, core: 2. Of those that a mesh axis runs over, the one named last changes fastest.
Arguments:
- solution: float32 [4, 192, 10240], P(None, 'gx', 'gy'), may hold values from -0.12 to 0.12
- forcing: float32 [4, 192, 10240], P(None, 'gx', 'gy'), may hold values from -0.12 to 0.12
- viscosity: float32 [192, 10240], P('gx', 'gy'), may hold values from 0.3 to 1
- blocks: float32 [16, 192, 10240], P(None, 'gx', 'gy'), may hold values from -0.5 to 0.5, as said below
- layer_count: int32 [192, 128], P('gx', 'gy'), may hold values from 40 to 80
- bed_frozen: int32 [192, 128], P('gx', 'gy'), may hold values 0 or 1
- basin_map: int32 [192, 128], P('gx', 'gy'), may hold values from 0 to 383, as said below
Outputs:
- smoothed: float32 [4, 192, 10240], P(None, 'gx', 'gy')
- column_residual: float32 [4, 192, 128], P(None, 'gx', 'gy')
- basin_residual: float32 [4, 384], replicated
Inputs may be any that keep to these rules, and one draw needn't show every extreme that they name: `blocks`: the first three diagonal entries of every cell's block are positive. `basin_map`: every basin number names some column.
All inputs are finite; a program needn't handle non-finite values. No bound on the sum of `bed_frozen` on one device may be relied on, other than what follows from the above.
Results may differ from a plain program's by a relative error of at most 0.00045.
Values sent between devices are 32-bit elements; how exact they have to be, the bound alone decides.
A program may use at most 64 MiB of HBM per device.

v0:
```python
import functools

import jax
import jax.numpy as jnp
from jax import lax
from jax.experimental import pallas as pl
from jax.experimental.pallas import tpu as pltpu
from jax.sharding import PartitionSpec as P

MESH = pl.DeviceIdType.MESH
HIGHEST = lax.Precision.HIGHEST
F32 = jnp.float32
LANE = 128


def factors(count_x):
    return (4, count_x // 8) if count_x == 96 else (2, count_x // 4)


def roll(value, shift, axis=1):
    size = value.shape[axis]
    return pltpu.roll(value, shift % size, axis)


def eliminate_levels(count):
    left = list(range(count))
    levels = []
    while len(left) > 1:
        gone = [pos for pos in range(0, len(left) - 1, 2)]
        levels.append([(left[p], left[p - 1] if p else None, left[p + 1]) for p in gone])
        left = [cell for pos, cell in enumerate(left) if pos not in gone]
    return levels


def solve_lines(load, store, count):
    sub = lax.broadcasted_iota(jnp.int32, (8, LANE), 0)
    first = sub == 0
    d0, d1, r0, r1 = ([load(t, q) for t in range(count)] for q in range(4))
    on0 = [d >= 0.0 for d in d0]
    on1 = [d >= 0.0 for d in d1]
    one, zero = jnp.full((8, LANE), 1.0, F32), jnp.zeros((8, LANE), F32)
    flag1 = [jnp.where(on, one, zero) for on in on1]
    before = [jnp.where(first, zero, roll(flag1[-1], 1, 0))] + flag1[:-1]
    edge_in = [jnp.where(on, b, zero) for on, b in zip(on0, before)]
    edge_mid = [jnp.where(on, f, zero) for on, f in zip(on0, flag1)]
    edge_out = edge_in[1:] + [roll(edge_in[0], -1, 0)]
    leak0 = [jnp.where(on, d + (2.0 - a - b), one) for on, d, a, b in zip(on0, d0, edge_in, edge_mid)]
    leak1 = [jnp.where(on, d + (2.0 - a - b), one) for on, d, a, b in zip(on1, d1, edge_mid, edge_out)]
    inv0 = [1.0 / (d + (a + b)) for d, a, b in zip(leak0, edge_in, edge_mid)]
    part_leak = [d * i for d, i in zip(leak0, inv0)]
    part_src = [r * i for r, i in zip(r0, inv0)]
    give_leak = [e * p for e, p in zip(edge_in, part_leak)]
    give_src = [e * p for e, p in zip(edge_in, part_src)]
    give_leak = give_leak[1:] + [roll(give_leak[0], -1, 0)]
    give_src = give_src[1:] + [roll(give_src[0], -1, 0)]
    leak = [d + (e * p + g) for d, e, p, g in zip(leak1, edge_mid, part_leak, give_leak)]
    src = [r + (e * p + g) for r, e, p, g in zip(r1, edge_mid, part_src, give_src)]
    edge = [a * (b * i) for a, b, i in zip(edge_in, edge_mid, inv0)]
    kept = {}
    for level in eliminate_levels(count):
        updates = []
        for cell, low, high in level:
            lo_edge, hi_edge = edge[cell], edge[high]
            inv = 1.0 / (leak[cell] + (lo_edge + hi_edge))
            lo_share, hi_share = lo_edge * inv, hi_edge * inv
            kept[cell] = (lo_share, hi_share, src[cell] * inv)
            updates.append((cell, low, high, lo_edge * hi_share, lo_share, hi_share))
        for cell, low, high, joined, lo_share, hi_share in updates:
            lo_leak, lo_src = lo_share * leak[cell], lo_share * src[cell]
            if low is None:
                low, lo_leak, lo_src = count - 1, roll(lo_leak, -1, 0), roll(lo_src, -1, 0)
            leak[low], src[low] = leak[low] + lo_leak, src[low] + lo_src
            leak[high], src[high] = leak[high] + hi_share * leak[cell], src[high] + hi_share * src[cell]
            edge[high] = joined
    last_leak, last_src, lo_edge = leak[-1], src[-1], edge[-1]
    hi_edge = roll(lo_edge, -1, 0)
    for hop in (1, 2, 4):
        inv = 1.0 / (last_leak + (lo_edge + hi_edge))
        p_leak, p_src, p_lo, p_hi = last_leak * inv, last_src * inv, lo_edge * inv, hi_edge * inv
        last_leak = last_leak + (lo_edge * roll(p_leak, hop, 0) + hi_edge * roll(p_leak, -hop, 0))
        last_src = last_src + (lo_edge * roll(p_src, hop, 0) + hi_edge * roll(p_src, -hop, 0))
        lo_edge, hi_edge = lo_edge * roll(p_lo, hop, 0), hi_edge * roll(p_hi, -hop, 0)
    value = [None] * count
    value[-1] = last_src / last_leak
    wrapped = roll(value[-1], 1, 0)
    for level in reversed(eliminate_levels(count)):
        for cell, low, high in level:
            lo_share, hi_share, own = kept[cell]
            lower = wrapped if low is None else value[low]
            value[cell] = own + (lo_share * lower + hi_share * value[high])
    for t in range(count):
        lower = wrapped if t == 0 else value[t - 1]
        store(t, 0, part_src[t] + (edge_in[t] * lower + edge_mid[t] * value[t]) * inv0[t])
        store(t, 1, value[t])


def sweep_kernel(
    count_x, count_y, basins,
    sol_ref, forc_ref, visc_ref, blk_ref, layers_ref, frozen_ref, basin_ref,
    smooth_ref, column_ref, total_ref,
    halo_out, halo_in, row_out, row_in, line_out, line_in,
    core_out, core_in, ring_buf, plane_buf, send_sem, recv_sem,
):
    cx, cz = factors(count_x)
    rows, lanes = visc_ref.shape
    y_cells = layers_ref.shape[1]
    layers = lanes // y_cells
    chunks = lanes // LANE
    owners = 3 * chunks
    seg = count_x // 8
    gx, gy = lax.axis_index("gx"), lax.axis_index("gy")
    core = lax.rem(gx, 2)
    pz = lax.rem(lax.div(gx, 2), cz)
    px = lax.div(gx, 2 * cz)
    partner = gx + 1 - 2 * core
    up_y = lax.rem(gy + 1, count_y)
    down_y = lax.rem(gy + count_y - 1, count_y)

    def plane_peer(i):
        x = lax.rem(px + lax.div(i, count_y), cx)
        y = lax.rem(gy + lax.rem(i, count_y), count_y)
        return x, y

    def gx_of(x, z, c):
        return (x * cz + z) * 2 + c

    barrier = pltpu.get_barrier_semaphore()

    def greet_line(i, carry):
        pl.semaphore_signal(barrier, inc=1, device_id=(lax.rem(gx + i, count_x), gy), device_id_type=MESH)
        return carry

    def greet_plane(i, carry):
        x = lax.rem(px + lax.div(i, count_y - 1), cx)
        y = lax.rem(gy + 1 + lax.rem(i, count_y - 1), count_y)
        pl.semaphore_signal(barrier, inc=1, device_id=(gx_of(x, pz, core), y), device_id_type=MESH)
        return carry

    lax.fori_loop(1, count_x, greet_line, 0)
    lax.fori_loop(0, cx * (count_y - 1), greet_plane, 0)

    def remote(src, dst, k, to):
        return pltpu.make_async_remote_copy(
            src_ref=src, dst_ref=dst, send_sem=send_sem.at[k], recv_sem=recv_sem.at[k],
            device_id=to, device_id_type=MESH,
        )

    def wait_rows(sem, ref, count):
        view = ref.at[pl.ds(0, count)]
        pltpu.make_async_copy(view, view, sem).wait()

    lane = lax.broadcasted_iota(jnp.int32, (rows, lanes), 1)

    def cell_of(index):
        return ((index.astype(F32) + 0.5) * (1.0 / layers)).astype(jnp.int32)

    layer = lane - cell_of(lane) * layers
    wide = lax.broadcasted_iota(jnp.int32, (y_cells, lanes), 1)
    spread = jnp.where(
        cell_of(wide) == lax.broadcasted_iota(jnp.int32, (y_cells, lanes), 0), 1.0, 0.0
    ).astype(F32)
    filled = jnp.dot(layers_ref[...].astype(F32), spread, precision=HIGHEST, preferred_element_type=F32)
    frozen = jnp.dot(frozen_ref[...].astype(F32), spread, precision=HIGHEST, preferred_element_type=F32)
    active = layer.astype(F32) + 0.5 < filled
    bottom, top = layer == 0, layer == layers - 1
    slide = 1.0 - frozen

    def masked(value):
        return jnp.where(active, value, 0.0)

    state = [masked(sol_ref[k]) for k in range(4)]
    small = lax.broadcasted_iota(jnp.int32, (rows, LANE), 1)

    def send_halo(values, k):
        for c in range(3):
            upward = jnp.where(small < layers, roll(values[c][:, lanes - LANE:], layers), 0.0)
            downward = jnp.where(small >= LANE - layers, roll(values[c][:, :LANE], LANE - layers), 0.0)
            halo_out[k, 0, pl.ds(c * rows, rows)] = upward
            halo_out[k, 1, pl.ds(c * rows, rows)] = downward
        up = remote(halo_out.at[k, 0], halo_in.at[k, 0], k * 2, (gx, up_y))
        down = remote(halo_out.at[k, 1], halo_in.at[k, 1], k * 2 + 1, (gx, down_y))
        up.start()
        down.start()
        return up, down

    def neighbours(values, k):
        out = []
        for c in range(3):
            v = values[c]
            low = jnp.where(gy > 0, halo_in[k, 0, pl.ds(c * rows, rows)], 0.0)
            high = jnp.where(gy < count_y - 1, halo_in[k, 1, pl.ds(c * rows, rows)], 0.0)
            before = jnp.where(lane < layers, 0.0, roll(v, layers))
            after = jnp.where(lane >= lanes - layers, 0.0, roll(v, lanes - layers))
            below = jnp.where(bottom, v * slide, roll(v, 1))
            above = jnp.where(top, 0.0, roll(v, lanes - 1))
            total = (before + after) + (below + above)
            if chunks > 1:
                pad = jnp.zeros((rows, lanes - LANE), F32)
                total = total + (jnp.concatenate([low, pad], 1) + jnp.concatenate([pad, high], 1))
            else:
                total = total + (low + high)
            out.append(total)
        return out

    def block(k, j):
        return blk_ref[4 * k + j]

    inv_visc = 1.0 / visc_ref[...]
    diag = [jnp.where(active, block(k, k) * inv_visc, -1.0) for k in range(3)]
    rest = []
    for k in range(3):
        acc = forc_ref[k]
        for j in range(4):
            if j != k:
                acc = acc - block(k, j) * state[j]
        rest.append(acc * inv_visc)

    pl.semaphore_wait(barrier, count_x - 1 + cx * (count_y - 1))
    first_halo = send_halo(state[:3], 0)
    for copy in first_halo:
        copy.wait_recv()
    around = neighbours(state[:3], 0)
    for k in range(3):
        rhs = masked(rest[k] + 0.25 * around[k])
        for j in range(chunks):
            at = (k * chunks + j) * 2 * rows
            row_out[pl.ds(at, rows)] = diag[k][:, j * LANE:(j + 1) * LANE]
            row_out[pl.ds(at + rows, rows)] = rhs[:, j * LANE:(j + 1) * LANE]

    wide_rows = 2 * rows

    def owner_of(q):
        return lax.div(q * count_x, owners)

    def to_owner(q, carry):
        to = owner_of(q)
        src = row_out.at[pl.ds(pl.multiple_of(q * wide_rows, wide_rows), wide_rows)]
        dst = row_in.at[pl.ds(pl.multiple_of(gx * wide_rows, wide_rows), wide_rows)]

        @pl.when(to == gx)
        def _():
            pltpu.make_async_copy(src, dst, recv_sem.at[4]).start()

        @pl.when(to != gx)
        def _():
            remote(src, dst, 4, (to, gy)).start()

        return carry

    lax.fori_loop(0, owners, to_owner, 0)
    mine = lax.div(owners * gx + count_x - 1, count_x)
    owning = jnp.logical_and(mine < owners, owner_of(mine) == gx)

    @pl.when(owning)
    def _():
        wait_rows(recv_sem.at[4], row_in, count_x * wide_rows)

        def load(t, q):
            return row_in[pl.ds(t * wide_rows + q, 8, stride=seg * wide_rows), :]

        def store(t, r, value):
            line_out[pl.ds(t * rows + r, 8, stride=seg * rows), :] = value

        solve_lines(load, store, seg)

        def give(i, carry):
            to = lax.rem(gx + i, count_x)
            src = line_out.at[pl.ds(pl.multiple_of(to * rows, rows), rows)]
            dst = line_in.at[pl.ds(pl.multiple_of(mine * rows, rows), rows)]

            @pl.when(i == count_x)
            def _():
                pltpu.make_async_copy(src, dst, recv_sem.at[5]).start()

            @pl.when(i != count_x)
            def _():
                remote(src, dst, 5, (to, gy)).start()

            return carry

        lax.fori_loop(1, count_x + 1, give, 0)

    eye = lax.broadcasted_iota(jnp.int32, (y_cells, y_cells), 0) == lax.broadcasted_iota(
        jnp.int32, (y_cells, y_cells), 1
    )
    names = basin_ref[...].astype(F32)
    wide_basins = basins
    basin_idx = lax.broadcasted_iota(jnp.int32, (y_cells, wide_basins), 1).astype(F32)
    member = []
    for x in range(rows):
        column = jnp.sum(jnp.where(eye, names[x:x + 1], 0.0), axis=1, keepdims=True)
        member.append(jnp.where(basin_idx == column, 1.0, 0.0).astype(F32))

    wait_rows(recv_sem.at[5], line_in, owners * rows)
    solved = [
        jnp.concatenate([line_in[pl.ds((k * chunks + j) * rows, rows)] for j in range(chunks)], 1)
        for k in range(3)
    ]
    change = [solved[k] - state[k] for k in range(3)]
    second_halo = send_halo(change, 1)
    acc = forc_ref[3] - block(3, 3) * state[3]
    for k in range(3):
        acc = acc - block(3, k) * solved[k]
    step = masked(acc * inv_visc)
    for k in range(3):
        smooth_ref[k] = jnp.where(active, solved[k], sol_ref[k])
    smooth_ref[3] = sol_ref[3] + step
    post = []
    for k in range(3):
        acc = block(k, 3) * step
        for j in range(3):
            if j != k:
                acc = acc + block(k, j) * change[j]
        post.append(acc)
    for copy in second_halo:
        copy.wait_recv()
    around = neighbours(change, 1)
    post = [masked(0.25 * visc_ref[...] * around[k] - post[k]) for k in range(3)]
    post.append((visc_ref[...] - block(3, 3)) * step)
    by_row = jnp.concatenate([post[k][x:x + 1] for x in range(rows) for k in range(4)], 0)
    sums = lax.dot_general(
        by_row, spread, (((1,), (1,)), ((), ())), precision=HIGHEST, preferred_element_type=F32
    )
    for x in range(rows):
        for k in range(4):
            column_ref[k, x:x + 1, :] = sums[4 * x + k:4 * x + k + 1]
    part = jnp.dot(sums[0:4], member[0], precision=HIGHEST, preferred_element_type=F32)
    for x in range(1, rows):
        part = part + jnp.dot(
            sums[4 * x:4 * x + 4], member[x], precision=HIGHEST, preferred_element_type=F32
        )

    pieces = wide_basins // LANE
    size = 2 * pieces

    def packed(pair):
        return jnp.concatenate([pair[:, j * LANE:(j + 1) * LANE] for j in range(pieces)], 0)

    lower, upper = packed(part[0:2]), packed(part[2:4])
    core_out[0] = jnp.where(core == 0, upper, lower)
    first = remote(core_out.at[0], core_in.at[0], 6, (partner, gy))
    first.start()
    first.wait_recv()
    own = jnp.where(core == 0, lower, upper) + core_in[0]
    ring_buf[pz] = own

    def to_ring(i, carry):
        z = lax.rem(pz + i, cz)
        remote(ring_buf.at[pz], ring_buf.at[pz], 7, (gx_of(px, z, core), gy)).start()
        return carry

    lax.fori_loop(1, cz, to_ring, 0)
    wait_rows(recv_sem.at[7], ring_buf, cz - 1)
    own = ring_buf[0]
    for i in range(1, cz):
        own = own + ring_buf[i]
    here = px * count_y + gy
    plane_buf[here] = own

    def to_plane(i, carry):
        x, y = plane_peer(i)
        remote(plane_buf.at[here], plane_buf.at[here], 8, (gx_of(x, pz, core), y)).start()
        return carry

    lax.fori_loop(1, cx * count_y, to_plane, 0)
    wait_rows(recv_sem.at[8], plane_buf, cx * count_y - 1)
    own = plane_buf[0]
    for i in range(1, cx * count_y):
        own = own + plane_buf[i]
    core_out[1] = own
    last = remote(core_out.at[1], core_in.at[1], 9, (partner, gy))
    last.start()
    last.wait_recv()
    other = core_in[1]
    lower, upper = jnp.where(core == 0, own, other), jnp.where(core == 0, other, own)
    for j in range(pieces):
        width = min(LANE, total_ref.shape[1] - j * LANE)
        if width > 0:
            total_ref[0:2, j * LANE:j * LANE + width] = lower[2 * j:2 * j + 2, :width]
            total_ref[2:4, j * LANE:j * LANE + width] = upper[2 * j:2 * j + 2, :width]

    for copy in first_halo + second_halo + (first, last):
        copy.wait_send()

    @pl.when(owning)
    def _():
        wait_rows(send_sem.at[4], row_out, (owners - 1) * wide_rows)
        wait_rows(send_sem.at[5], line_out, (count_x - 1) * rows)

    @pl.when(jnp.logical_not(owning))
    def _():
        wait_rows(send_sem.at[4], row_out, owners * wide_rows)

    wait_rows(send_sem.at[7], ring_buf, cz - 1)
    wait_rows(send_sem.at[8], plane_buf, cx * count_y - 1)


def solution(mesh):
    count_x, count_y = mesh.shape["gx"], mesh.shape["gy"]
    cx, cz = factors(count_x)

    def local(sol, forc, visc, blocks, layers, frozen, basin_map):
        rows, lanes = visc.shape
        chunks = lanes // LANE
        owners = 3 * chunks
        basins = count_x // 2 * count_y
        padded = -(-basins // LANE) * LANE
        size = 2 * padded // LANE
        vmem = pl.BlockSpec(memory_space=pltpu.VMEM)
        return pl.pallas_call(
            functools.partial(sweep_kernel, count_x, count_y, padded),
            out_shape=(
                jax.ShapeDtypeStruct(sol.shape, F32),
                jax.ShapeDtypeStruct((4,) + layers.shape, F32),
                jax.ShapeDtypeStruct((4, basins), F32),
            ),
            in_specs=[vmem] * 7,
            out_specs=(vmem, vmem, vmem),
            scratch_shapes=[
                pltpu.VMEM((2, 2, 8, LANE), F32),
                pltpu.VMEM((2, 2, 8, LANE), F32),
                pltpu.VMEM((owners * 2 * rows, LANE), F32),
                pltpu.VMEM((count_x * 2 * rows, LANE), F32),
                pltpu.VMEM((count_x * rows, LANE), F32),
                pltpu.VMEM((owners * rows, LANE), F32),
                pltpu.VMEM((2, size, LANE), F32),
                pltpu.VMEM((2, size, LANE), F32),
                pltpu.VMEM((cz, size, LANE), F32),
                pltpu.VMEM((cx * count_y, size, LANE), F32),
                pltpu.SemaphoreType.DMA((10,)),
                pltpu.SemaphoreType.DMA((10,)),
            ],
            compiler_params=pltpu.CompilerParams(
                collective_id=0, has_side_effects=True, vmem_limit_bytes=32 * 2**20
            ),
            name="sweep",
        )(sol, forc, visc, blocks, layers, frozen, basin_map)

    return jax.shard_map(
        local,
        mesh=mesh,
        in_specs=(
            P(None, "gx", "gy"), P(None, "gx", "gy"), P("gx", "gy"), P(None, "gx", "gy"),
            P("gx", "gy"), P("gx", "gy"), P("gx", "gy"),
        ),
        out_specs=(P(None, "gx", "gy"), P(None, "gx", "gy"), P()),
        check_vma=False,
    )
```

profile of v0, /device:TPU:1, one launch (start us, length us, event | category | flops | bytes accessed | tf_op | source)
XLA Modules:
  0.0 67.7 jit_solution(11120021344049456413)
XLA Ops:
  0.6 0.0 copy-start
  0.6 0.9 %copy-done = f32[16,2,1280]{2,1,0:T(2,128)S(1)} copy-done((f32[16,2,1280]{2,1,0:T(2,128)S(1)}, f32[16,2,1280]{2,1,0:T(2,128)}, u32[]{:S(2)}) %copy-start) | copy-done | bytes 163864
  1.5 0.0 copy-start.1
  1.6 0.8 %copy-done.1 = f32[4,2,1280]{2,1,0:T(2,128)S(1)} copy-done((f32[4,2,1280]{2,1,0:T(2,128)S(1)}, f32[4,2,1280]{2,1,0:T(2,128)}, u32[]{:S(2)}) %copy-start.1) | copy-done | bytes 40984
  2.3 0.0 copy-start.2
  2.3 0.8 %copy-done.2 = f32[4,2,1280]{2,1,0:T(2,128)S(1)} copy-done((f32[4,2,1280]{2,1,0:T(2,128)S(1)}, f32[4,2,1280]{2,1,0:T(2,128)}, u32[]{:S(2)}) %copy-start.2) | copy-done | bytes 40984
  3.1 0.0 copy-start.3
  3.1 0.7 %copy-done.3 = f32[2,1280]{1,0:T(2,128)S(1)} copy-done((f32[2,1280]{1,0:T(2,128)S(1)}, f32[2,1280]{1,0:T(2,128)}, u32[]{:S(2)}) %copy-start.3) | copy-done | bytes 10264
  3.8 0.0 copy-start.4
  3.8 0.7 copy-done.4
  4.5 0.0 copy-start.5
  4.5 0.7 copy-done.5
  5.2 0.0 copy-start.6
  5.2 0.7 copy-done.6
  5.8 60.1 %sweep.1 = (f32[4,2,1280]{2,1,0:T(2,128)S(1)}, f32[4,2,16]{2,1,0:T(2,128)S(1)}, f32[4,384]{1,0:T(4,128)S(1)}) custom-call(f32[4,2,1280]{2,1,0:T(2,128)S(1)} %copy-done.1, f32[4,2,1280]{2,1,0:T(2,128)S(1)} %copy-done.2, f32[2,1280]{1,0:T(2,128)S(1)} %copy-done.3, f32[16,2,1280]{2,1,0:T(2,128)S(1)} %copy-done, s32[2,16]{1,0:T(2,128)S(1)} %copy-done.4, ...), custom_call_target="tpu_custom_call" | custom-call | tf_op jit(solution)/shard_map/sweep/pallas_call | solution.py:410
  65.9 0.6 copy.13
  66.5 0.6 copy.14
  67.1 0.6 copy.15
Async XLA Ops:
  0.6 0.9 %copy-start = (f32[16,2,1280]{2,1,0:T(2,128)S(1)}, f32[16,2,1280]{2,1,0:T(2,128)}, u32[]{:S(2)}) copy-start(f32[16,2,1280]{2,1,0:T(2,128)} %blk_ref.1) | copy-start | bytes 491524
  1.5 0.8 %copy-start.1 = (f32[4,2,1280]{2,1,0:T(2,128)S(1)}, f32[4,2,1280]{2,1,0:T(2,128)}, u32[]{:S(2)}) copy-start(f32[4,2,1280]{2,1,0:T(2,128)} %sol_ref.1) | copy-start | bytes 122884
  2.3 0.8 %copy-start.2 = (f32[4,2,1280]{2,1,0:T(2,128)S(1)}, f32[4,2,1280]{2,1,0:T(2,128)}, u32[]{:S(2)}) copy-start(f32[4,2,1280]{2,1,0:T(2,128)} %forc_ref.1) | copy-start | bytes 122884
  3.1 0.7 %copy-start.3 = (f32[2,1280]{1,0:T(2,128)S(1)}, f32[2,1280]{1,0:T(2,128)}, u32[]{:S(2)}) copy-start(f32[2,1280]{1,0:T(2,128)} %visc_ref.1) | copy-start | bytes 30724
  3.8 0.7 %copy-start.4 = (s32[2,16]{1,0:T(2,128)S(1)}, s32[2,16]{1,0:T(2,128)}, u32[]{:S(2)}) copy-start(s32[2,16]{1,0:T(2,128)} %layers_ref.1) | copy-start | bytes 388
  4.5 0.7 %copy-start.5 = (s32[2,16]{1,0:T(2,128)S(1)}, s32[2,16]{1,0:T(2,128)}, u32[]{:S(2)}) copy-start(s32[2,16]{1,0:T(2,128)} %frozen_ref.1) | copy-start | bytes 388
  5.2 0.7 %copy-start.6 = (s32[2,16]{1,0:T(2,128)S(1)}, s32[2,16]{1,0:T(2,128)}, u32[]{:S(2)}) copy-start(s32[2,16]{1,0:T(2,128)} %basin_ref.1) | copy-start | bytes 388
where the time goes:
time: 68.1 us; the launch traced here: 67.7 us
  Pallas kernels  60.1 us (88%)
  local copies, waits for them, and re-layouts  7.01 us (10%)
    pallas_call x1, Pallas kernels, local(): pl.pallas_call(functools.partial(sweep_kernel, count_x, count_y, padded),...  60.1 us
    unnamed x17, local copies, waits for them, and re-layouts  7.01 us

commit v1 on v0

--- a/solution.py
+++ b/solution.py
@@ -39,6 +39,8 @@
     on0 = [d >= 0.0 for d in d0]
     on1 = [d >= 0.0 for d in d1]
     one, zero = jnp.full((8, LANE), 1.0, F32), jnp.zeros((8, LANE), F32)
+    r0 = [jnp.where(on, r, zero) for on, r in zip(on0, r0)]
+    r1 = [jnp.where(on, r, zero) for on, r in zip(on1, r1)]
     flag1 = [jnp.where(on, one, zero) for on in on1]
     before = [jnp.where(first, zero, roll(flag1[-1], 1, 0))] + flag1[:-1]
     edge_in = [jnp.where(on, b, zero) for on, b in zip(on0, before)]
@@ -94,12 +96,18 @@
         store(t, 1, value[t])
 
 
+def far_first(i, count):
+    side = 1 - 2 * lax.rem(i, 2)
+    return count // 2 + side * lax.div(i + 1, 2)
+
+
 def sweep_kernel(
     count_x, count_y, basins,
+    sol_hbm, forc_hbm, visc_hbm, blk_hbm, layers_hbm, frozen_hbm, basin_hbm,
+    smooth_ref, column_ref, total_ref,
     sol_ref, forc_ref, visc_ref, blk_ref, layers_ref, frozen_ref, basin_ref,
-    smooth_ref, column_ref, total_ref,
-    halo_out, halo_in, row_out, row_in, line_out, line_in,
-    core_out, core_in, ring_buf, plane_buf, send_sem, recv_sem,
+    edge_out, edge_in, halo_out, halo_in, row_out, row_in, line_out, line_in,
+    core_out, core_in, ring_buf, plane_buf, load_sem, send_sem, recv_sem, ready_sem,
 ):
     cx, cz = factors(count_x)
     rows, lanes = visc_ref.shape
@@ -108,36 +116,60 @@
     chunks = lanes // LANE
     owners = 3 * chunks
     seg = count_x // 8
+    z_step = 2 if cz >= 8 else 1
+    z_owning = -(-owners // (2 * cx))
     gx, gy = lax.axis_index("gx"), lax.axis_index("gy")
     core = lax.rem(gx, 2)
     pz = lax.rem(lax.div(gx, 2), cz)
     px = lax.div(gx, 2 * cz)
     partner = gx + 1 - 2 * core
-    up_y = lax.rem(gy + 1, count_y)
-    down_y = lax.rem(gy + count_y - 1, count_y)
-
-    def plane_peer(i):
-        x = lax.rem(px + lax.div(i, count_y), cx)
-        y = lax.rem(gy + lax.rem(i, count_y), count_y)
-        return x, y
+    mine = (lax.div(pz, z_step) * cx + px) * 2 + core
+    owning = jnp.logical_and(lax.rem(pz, z_step) == 0, mine < owners)
+    my_chunk = lax.rem(mine, chunks)
+    low_edge = jnp.logical_and(owning, my_chunk == 0)
+    high_edge = jnp.logical_and(owning, my_chunk == chunks - 1)
+
+    def along_y(step):
+        return lax.rem(gy + step + count_y, count_y)
 
     def gx_of(x, z, c):
         return (x * cz + z) * 2 + c
 
+    def owner_of(q):
+        return gx_of(lax.rem(lax.div(q, 2), cx), lax.div(q, 2 * cx) * z_step, lax.rem(q, 2))
+
+    loads = [
+        pltpu.make_async_copy(src, dst, load_sem.at[i])
+        for i, (src, dst) in enumerate((
+            (layers_hbm, layers_ref), (frozen_hbm, frozen_ref), (sol_hbm, sol_ref),
+            (visc_hbm, visc_ref), (blk_hbm, blk_ref), (forc_hbm, forc_ref), (basin_hbm, basin_ref),
+        ))
+    ]
+    for copy in loads:
+        copy.start()
+
     barrier = pltpu.get_barrier_semaphore()
 
-    def greet_line(i, carry):
-        pl.semaphore_signal(barrier, inc=1, device_id=(lax.rem(gx + i, count_x), gy), device_id_type=MESH)
-        return carry
-
-    def greet_plane(i, carry):
-        x = lax.rem(px + lax.div(i, count_y - 1), cx)
-        y = lax.rem(gy + 1 + lax.rem(i, count_y - 1), count_y)
-        pl.semaphore_signal(barrier, inc=1, device_id=(gx_of(x, pz, core), y), device_id_type=MESH)
-        return carry
-
-    lax.fori_loop(1, count_x, greet_line, 0)
-    lax.fori_loop(0, cx * (count_y - 1), greet_plane, 0)
+    def greet(y):
+        def one(i, carry):
+            pl.semaphore_signal(
+                barrier, inc=1, device_id=(lax.rem(gx + i, count_x), y), device_id_type=MESH
+            )
+            return carry
+
+        return one
+
+    @pl.when(owning)
+    def _():
+        lax.fori_loop(1, count_x, greet(gy), 0)
+
+    @pl.when(low_edge)
+    def _():
+        lax.fori_loop(0, count_x, greet(along_y(-1)), 0)
+
+    @pl.when(high_edge)
+    def _():
+        lax.fori_loop(0, count_x, greet(along_y(1)), 0)
 
     def remote(src, dst, k, to):
         return pltpu.make_async_remote_copy(
@@ -159,6 +191,8 @@
     spread = jnp.where(
         cell_of(wide) == lax.broadcasted_iota(jnp.int32, (y_cells, lanes), 0), 1.0, 0.0
     ).astype(F32)
+    loads[0].wait()
+    loads[1].wait()
     filled = jnp.dot(layers_ref[...].astype(F32), spread, precision=HIGHEST, preferred_element_type=F32)
     frozen = jnp.dot(frozen_ref[...].astype(F32), spread, precision=HIGHEST, preferred_element_type=F32)
     active = layer.astype(F32) + 0.5 < filled
@@ -168,95 +202,110 @@
     def masked(value):
         return jnp.where(active, value, 0.0)
 
+    loads[2].wait()
     state = [masked(sol_ref[k]) for k in range(4)]
     small = lax.broadcasted_iota(jnp.int32, (rows, LANE), 1)
 
-    def send_halo(values, k):
-        for c in range(3):
-            upward = jnp.where(small < layers, roll(values[c][:, lanes - LANE:], layers), 0.0)
-            downward = jnp.where(small >= LANE - layers, roll(values[c][:, :LANE], LANE - layers), 0.0)
-            halo_out[k, 0, pl.ds(c * rows, rows)] = upward
-            halo_out[k, 1, pl.ds(c * rows, rows)] = downward
-        up = remote(halo_out.at[k, 0], halo_in.at[k, 0], k * 2, (gx, up_y))
-        down = remote(halo_out.at[k, 1], halo_in.at[k, 1], k * 2 + 1, (gx, down_y))
-        up.start()
-        down.start()
-        return up, down
-
-    def neighbours(values, k):
+    def facing_up(value):
+        return jnp.where(small < layers, roll(value[:, lanes - LANE:], layers), 0.0)
+
+    def facing_down(value):
+        return jnp.where(small >= LANE - layers, roll(value[:, :LANE], LANE - layers), 0.0)
+
+    def inner_neighbours(values):
         out = []
-        for c in range(3):
-            v = values[c]
-            low = jnp.where(gy > 0, halo_in[k, 0, pl.ds(c * rows, rows)], 0.0)
-            high = jnp.where(gy < count_y - 1, halo_in[k, 1, pl.ds(c * rows, rows)], 0.0)
+        for v in values:
             before = jnp.where(lane < layers, 0.0, roll(v, layers))
             after = jnp.where(lane >= lanes - layers, 0.0, roll(v, lanes - layers))
             below = jnp.where(bottom, v * slide, roll(v, 1))
             above = jnp.where(top, 0.0, roll(v, lanes - 1))
-            total = (before + after) + (below + above)
-            if chunks > 1:
-                pad = jnp.zeros((rows, lanes - LANE), F32)
-                total = total + (jnp.concatenate([low, pad], 1) + jnp.concatenate([pad, high], 1))
-            else:
-                total = total + (low + high)
-            out.append(total)
+            out.append((before + after) + (below + above))
         return out
 
     def block(k, j):
         return blk_ref[4 * k + j]
 
+    for k in range(3):
+        edge_out[pl.ds((2 * k) * rows, rows)] = facing_up(state[k])
+        edge_out[pl.ds((2 * k + 1) * rows, rows)] = facing_down(state[k])
+    around = inner_neighbours(state[:3])
+    wide_rows = 2 * rows
+    loads[3].wait()
+    loads[4].wait()
+    loads[5].wait()
     inv_visc = 1.0 / visc_ref[...]
-    diag = [jnp.where(active, block(k, k) * inv_visc, -1.0) for k in range(3)]
-    rest = []
     for k in range(3):
         acc = forc_ref[k]
         for j in range(4):
             if j != k:
                 acc = acc - block(k, j) * state[j]
-        rest.append(acc * inv_visc)
-
-    pl.semaphore_wait(barrier, count_x - 1 + cx * (count_y - 1))
-    first_halo = send_halo(state[:3], 0)
-    for copy in first_halo:
-        copy.wait_recv()
-    around = neighbours(state[:3], 0)
-    for k in range(3):
-        rhs = masked(rest[k] + 0.25 * around[k])
+        rhs = masked(acc * inv_visc + 0.25 * around[k])
+        diag = jnp.where(active, block(k, k) * inv_visc, -1.0)
         for j in range(chunks):
-            at = (k * chunks + j) * 2 * rows
-            row_out[pl.ds(at, rows)] = diag[k][:, j * LANE:(j + 1) * LANE]
+            at = (k * chunks + j) * wide_rows
+            row_out[pl.ds(at, rows)] = diag[:, j * LANE:(j + 1) * LANE]
             row_out[pl.ds(at + rows, rows)] = rhs[:, j * LANE:(j + 1) * LANE]
 
-    wide_rows = 2 * rows
-
-    def owner_of(q):
-        return lax.div(q * count_x, owners)
-
-    def to_owner(q, carry):
+    @pl.when(owning)
+    def _():
+        pl.semaphore_wait(barrier, owners + 6 - 1)
+
+    @pl.when(jnp.logical_not(owning))
+    def _():
+        pl.semaphore_wait(barrier, owners + 6)
+
+    for k in range(3):
+        for side, step, chunk in ((0, 1, 0), (1, -1, chunks - 1)):
+            remote(
+                edge_out.at[pl.ds((2 * k + side) * rows, rows)],
+                edge_in.at[side, pl.ds(pl.multiple_of(gx * rows, rows), rows)],
+                side, (owner_of(k * chunks + chunk), along_y(step)),
+            ).start()
+
+    def to_owner(i, carry):
+        x = lax.rem(px + far_first(lax.rem(lax.div(i, 2), cx), cx), cx)
+        q = ((z_owning - 1 - lax.div(i, 2 * cx)) * cx + x) * 2 + lax.rem(i, 2)
         to = owner_of(q)
-        src = row_out.at[pl.ds(pl.multiple_of(q * wide_rows, wide_rows), wide_rows)]
+        at = jnp.minimum(q, owners - 1)
+        src = row_out.at[pl.ds(pl.multiple_of(at * wide_rows, wide_rows), wide_rows)]
         dst = row_in.at[pl.ds(pl.multiple_of(gx * wide_rows, wide_rows), wide_rows)]
 
         @pl.when(to == gx)
         def _():
-            pltpu.make_async_copy(src, dst, recv_sem.at[4]).start()
-
-        @pl.when(to != gx)
+            @pl.when(q < owners)
+            def _():
+                pltpu.make_async_copy(src, dst, recv_sem.at[4]).start()
+
+        @pl.when(jnp.logical_and(to != gx, q < owners))
         def _():
             remote(src, dst, 4, (to, gy)).start()
 
         return carry
 
-    lax.fori_loop(0, owners, to_owner, 0)
-    mine = lax.div(owners * gx + count_x - 1, count_x)
-    owning = jnp.logical_and(mine < owners, owner_of(mine) == gx)
+    lax.fori_loop(0, 2 * cx * z_owning, to_owner, 0)
 
     @pl.when(owning)
     def _():
+        @pl.when(low_edge)
+        def _():
+            wait_rows(recv_sem.at[0], edge_in.at[0], count_x * rows)
+
+        @pl.when(high_edge)
+        def _():
+            wait_rows(recv_sem.at[1], edge_in.at[1], count_x * rows)
+
         wait_rows(recv_sem.at[4], row_in, count_x * wide_rows)
+        low_on = jnp.logical_and(my_chunk == 0, gy > 0)
+        high_on = jnp.logical_and(my_chunk == chunks - 1, gy < count_y - 1)
 
         def load(t, q):
-            return row_in[pl.ds(t * wide_rows + q, 8, stride=seg * wide_rows), :]
+            value = row_in[pl.ds(t * wide_rows + q, 8, stride=seg * wide_rows), :]
+            if q >= rows:
+                at = pl.ds(t * rows + q - rows, 8, stride=seg * rows)
+                low = jnp.where(low_on, edge_in[0, at, :], 0.0)
+                high = jnp.where(high_on, edge_in[1, at, :], 0.0)
+                value = value + 0.25 * (low + high)
+            return value
 
         def store(t, r, value):
             line_out[pl.ds(t * rows + r, 8, stride=seg * rows), :] = value
@@ -264,28 +313,30 @@
         solve_lines(load, store, seg)
 
         def give(i, carry):
-            to = lax.rem(gx + i, count_x)
+            z = lax.rem(pz + far_first(lax.div(i, 2 * cx), cz), cz)
+            x = lax.rem(px + far_first(lax.rem(lax.div(i, 2), cx), cx), cx)
+            to = gx_of(x, z, lax.rem(i, 2))
             src = line_out.at[pl.ds(pl.multiple_of(to * rows, rows), rows)]
             dst = line_in.at[pl.ds(pl.multiple_of(mine * rows, rows), rows)]
 
-            @pl.when(i == count_x)
+            @pl.when(to == gx)
             def _():
                 pltpu.make_async_copy(src, dst, recv_sem.at[5]).start()
 
-            @pl.when(i != count_x)
+            @pl.when(to != gx)
             def _():
                 remote(src, dst, 5, (to, gy)).start()
 
             return carry
 
-        lax.fori_loop(1, count_x + 1, give, 0)
-
+        lax.fori_loop(0, count_x, give, 0)
+
+    loads[6].wait()
     eye = lax.broadcasted_iota(jnp.int32, (y_cells, y_cells), 0) == lax.broadcasted_iota(
         jnp.int32, (y_cells, y_cells), 1
     )
     names = basin_ref[...].astype(F32)
-    wide_basins = basins
-    basin_idx = lax.broadcasted_iota(jnp.int32, (y_cells, wide_basins), 1).astype(F32)
+    basin_idx = lax.broadcasted_iota(jnp.int32, (y_cells, basins), 1).astype(F32)
     member = []
     for x in range(rows):
         column = jnp.sum(jnp.where(eye, names[x:x + 1], 0.0), axis=1, keepdims=True)
@@ -297,7 +348,30 @@
         for k in range(3)
     ]
     change = [solved[k] - state[k] for k in range(3)]
-    second_halo = send_halo(change, 1)
+
+    halos = []
+    for side, step in ((0, 1), (1, -1)):
+        for c in range(3):
+            facing = facing_up if side == 0 else facing_down
+            halo_out[side, pl.ds(c * rows, rows)] = facing(change[c])
+        copy = remote(halo_out.at[side], halo_in.at[side], 2 + side, (gx, along_y(step)))
+        copy.start()
+        halos.append(copy)
+
+    reach = 1
+    rounds = []
+    while reach < count_y // 2:
+        rounds.append(reach)
+        reach *= 2
+
+    def tell(k):
+        for step in (rounds[k], -rounds[k]):
+            pl.semaphore_signal(
+                ready_sem.at[k], inc=1, device_id=(gx, along_y(step)), device_id_type=MESH
+            )
+
+    if rounds:
+        tell(0)
     acc = forc_ref[3] - block(3, 3) * state[3]
     for k in range(3):
         acc = acc - block(3, k) * solved[k]
@@ -305,17 +379,23 @@
     for k in range(3):
         smooth_ref[k] = jnp.where(active, solved[k], sol_ref[k])
     smooth_ref[3] = sol_ref[3] + step
-    post = []
+    around = inner_neighbours(change)
+    coupled = []
     for k in range(3):
         acc = block(k, 3) * step
         for j in range(3):
             if j != k:
                 acc = acc + block(k, j) * change[j]
-        post.append(acc)
-    for copy in second_halo:
+        coupled.append(acc)
+    for copy in halos:
         copy.wait_recv()
-    around = neighbours(change, 1)
-    post = [masked(0.25 * visc_ref[...] * around[k] - post[k]) for k in range(3)]
+    post = []
+    for k in range(3):
+        low = jnp.where(gy > 0, halo_in[0, pl.ds(k * rows, rows)], 0.0)
+        high = jnp.where(gy < count_y - 1, halo_in[1, pl.ds(k * rows, rows)], 0.0)
+        pad = jnp.zeros((rows, lanes - LANE), F32)
+        beside = jnp.concatenate([low, pad], 1) + jnp.concatenate([pad, high], 1)
+        post.append(masked(0.25 * visc_ref[...] * (around[k] + beside) - coupled[k]))
     post.append((visc_ref[...] - block(3, 3)) * step)
     by_row = jnp.concatenate([post[k][x:x + 1] for x in range(rows) for k in range(4)], 0)
     sums = lax.dot_general(
@@ -330,8 +410,7 @@
             sums[4 * x:4 * x + 4], member[x], precision=HIGHEST, preferred_element_type=F32
         )
 
-    pieces = wide_basins // LANE
-    size = 2 * pieces
+    pieces = basins // LANE
 
     def packed(pair):
         return jnp.concatenate([pair[:, j * LANE:(j + 1) * LANE] for j in range(pieces)], 0)
@@ -340,29 +419,38 @@
     core_out[0] = jnp.where(core == 0, upper, lower)
     first = remote(core_out.at[0], core_in.at[0], 6, (partner, gy))
     first.start()
+    if rounds:
+        pl.semaphore_wait(ready_sem.at[0], 2)
+        for k in range(1, len(rounds)):
+            tell(k)
+            if k + 1 < len(rounds):
+                pl.semaphore_wait(ready_sem.at[k], 2)
     first.wait_recv()
     own = jnp.where(core == 0, lower, upper) + core_in[0]
     ring_buf[pz] = own
 
     def to_ring(i, carry):
-        z = lax.rem(pz + i, cz)
+        z = lax.rem(pz + far_first(i, cz), cz)
         remote(ring_buf.at[pz], ring_buf.at[pz], 7, (gx_of(px, z, core), gy)).start()
         return carry
 
-    lax.fori_loop(1, cz, to_ring, 0)
+    lax.fori_loop(0, cz - 1, to_ring, 0)
     wait_rows(recv_sem.at[7], ring_buf, cz - 1)
     own = ring_buf[0]
     for i in range(1, cz):
         own = own + ring_buf[i]
+    if len(rounds) > 1:
+        pl.semaphore_wait(ready_sem.at[len(rounds) - 1], 2)
     here = px * count_y + gy
     plane_buf[here] = own
 
     def to_plane(i, carry):
-        x, y = plane_peer(i)
+        x = lax.rem(px + far_first(lax.rem(i, cx), cx), cx)
+        y = lax.rem(gy + far_first(lax.div(i, cx), count_y), count_y)
         remote(plane_buf.at[here], plane_buf.at[here], 8, (gx_of(x, pz, core), y)).start()
         return carry
 
-    lax.fori_loop(1, cx * count_y, to_plane, 0)
+    lax.fori_loop(0, cx * count_y - 1, to_plane, 0)
     wait_rows(recv_sem.at[8], plane_buf, cx * count_y - 1)
     own = plane_buf[0]
     for i in range(1, cx * count_y):
@@ -379,8 +467,10 @@
             total_ref[0:2, j * LANE:j * LANE + width] = lower[2 * j:2 * j + 2, :width]
             total_ref[2:4, j * LANE:j * LANE + width] = upper[2 * j:2 * j + 2, :width]
 
-    for copy in first_halo + second_halo + (first, last):
+    for copy in halos + [first, last]:
         copy.wait_send()
+    for side in range(2):
+        wait_rows(send_sem.at[side], edge_out, 3 * rows)
 
     @pl.when(owning)
     def _():
@@ -407,18 +497,23 @@
         padded = -(-basins // LANE) * LANE
         size = 2 * padded // LANE
         vmem = pl.BlockSpec(memory_space=pltpu.VMEM)
+        anywhere = pl.BlockSpec(memory_space=pl.ANY)
+        results = (
+            jax.ShapeDtypeStruct(sol.shape, F32),
+            jax.ShapeDtypeStruct((4,) + layers.shape, F32),
+            jax.ShapeDtypeStruct((4, basins), F32),
+        )
+        inputs = (sol, forc, visc, blocks, layers, frozen, basin_map)
         return pl.pallas_call(
             functools.partial(sweep_kernel, count_x, count_y, padded),
-            out_shape=(
-                jax.ShapeDtypeStruct(sol.shape, F32),
-                jax.ShapeDtypeStruct((4,) + layers.shape, F32),
-                jax.ShapeDtypeStruct((4, basins), F32),
-            ),
-            in_specs=[vmem] * 7,
+            out_shape=results,
+            in_specs=[anywhere] * 7,
             out_specs=(vmem, vmem, vmem),
-            scratch_shapes=[
-                pltpu.VMEM((2, 2, 8, LANE), F32),
-                pltpu.VMEM((2, 2, 8, LANE), F32),
+            scratch_shapes=[pltpu.VMEM(a.shape, a.dtype) for a in inputs] + [
+                pltpu.VMEM((6 * rows, LANE), F32),
+                pltpu.VMEM((2, count_x * rows, LANE), F32),
+                pltpu.VMEM((2, 3 * rows, LANE), F32),
+                pltpu.VMEM((2, 3 * rows, LANE), F32),
                 pltpu.VMEM((owners * 2 * rows, LANE), F32),
                 pltpu.VMEM((count_x * 2 * rows, LANE), F32),
                 pltpu.VMEM((count_x * rows, LANE), F32),
@@ -427,15 +522,16 @@
                 pltpu.VMEM((2, size, LANE), F32),
                 pltpu.VMEM((cz, size, LANE), F32),
                 pltpu.VMEM((cx * count_y, size, LANE), F32),
+                pltpu.SemaphoreType.DMA((7,)),
                 pltpu.SemaphoreType.DMA((10,)),
                 pltpu.SemaphoreType.DMA((10,)),
+                pltpu.SemaphoreType.REGULAR((4,)),
             ],
             compiler_params=pltpu.CompilerParams(
-                collective_id=0, has_side_effects=True, vmem_limit_bytes=32 * 2**20
+                collective_id=0, has_side_effects=True, vmem_limit_bytes=63 * 2**20
             ),
             name="sweep",
-        )(sol, forc, visc, blocks, layers, frozen, basin_map)
-
+        )(*inputs)
     return jax.shard_map(
         local,
         mesh=mesh,

time: 68.1 us -> 59.5 us (0.87)
  local copies, waits for them, and re-layouts: 7.01 us -> 2.69 us
  Pallas kernels: 60.1 us -> 55.9 us
    unnamed x17 -> x7, local copies, waits for them, and re-layouts: 7.01 us -> 2.69 us
    pallas_call x1, Pallas kernels: 60.1 us -> 55.9 us  [local(): pl.pallas_call(functools.partial(sweep_kernel, count_x, count_y, padded),...]
where the time goes in v1:
time: 59.5 us; the launch traced here: 59.3 us
  Pallas kernels  55.9 us (94%)
  local copies, waits for them, and re-layouts  2.69 us (5%)
  between operations  0.65 us (1%)
    pallas_call x1, Pallas kernels, local(): pl.pallas_call(functools.partial(sweep_kernel, count_x, count_y, padded),...  55.9 us
    unnamed x7, local copies, waits for them, and re-layouts  2.69 us

profile of v1, /device:TPU:1, one launch (start us, length us, event | category | flops | bytes accessed | tf_op | source)
XLA Modules:
  0.0 59.3 jit_solution(6606908778801491949)
XLA Ops:
  0.6 55.9 %sweep.1 = (f32[4,2,1280]{2,1,0:T(2,128)}, f32[4,2,16]{2,1,0:T(2,128)}, f32[4,384]{1,0:T(4,128)}) custom-call(f32[4,2,1280]{2,1,0:T(2,128)} %sol_hbm.1, f32[4,2,1280]{2,1,0:T(2,128)} %forc_hbm.1, f32[2,1280]{1,0:T(2,128)} %visc_hbm.1, f32[16,2,1280]{2,1,0:T(2,128)} %blk_hbm.1, s32[2,16]{1,0:T(2,128)} %layers_hbm.1, s32[2,16]{1,0:T(2,128)} %frozen_hbm.1, ...), custom_call_target="tpu_custom_call" | custom-call | tf_op jit(solution)/shard_map/sweep/pallas_call | solution.py:507
  56.6 0.0 copy-start.1
  56.6 1.4 %copy.13 = f32[4,2,1280]{2,1,0:T(2,128)} copy(f32[4,2,1280]{2,1,0:T(2,128)} %get-tuple-element.6) | data formatting | bytes 81920
  58.0 0.0 copy-done.1
  58.0 0.0 copy-start
  58.0 0.6 copy.14
  58.6 0.1 copy-done
  58.7 0.6 copy.15
Async XLA Ops:
  56.6 1.4 %copy-start.1 = (f32[4,2,16]{2,1,0:T(2,128)S(1)}, f32[4,2,16]{2,1,0:T(2,128)}, u32[]{:S(2)}) copy-start(f32[4,2,16]{2,1,0:T(2,128)} %get-tuple-element.7) | copy-start | bytes 1540
  58.0 0.7 %copy-start = (f32[4,384]{1,0:T(4,128)S(1)}, f32[4,384]{1,0:T(4,128)}, u32[]{:S(2)}) copy-start(f32[4,384]{1,0:T(4,128)} %get-tuple-element.8) | copy-start | bytes 18436

commit v2 on v1

v2 whole, which is shorter than its diff:
```python
import functools

import jax
import jax.numpy as jnp
from jax import lax
from jax.experimental import pallas as pl
from jax.experimental.pallas import tpu as pltpu
from jax.sharding import PartitionSpec as P

MESH = pl.DeviceIdType.MESH
HIGHEST = lax.Precision.HIGHEST
F32 = jnp.float32
LANE = 128
SKIP = 3


def factors(count_x):
    return (4, count_x // 8) if count_x == 96 else (2, count_x // 4)


def roll(value, shift, axis=1):
    size = value.shape[axis]
    return pltpu.roll(value, shift % size, axis)


def eliminate_levels(count):
    left = list(range(count))
    levels = []
    while len(left) > 1:
        gone = [pos for pos in range(0, len(left) - 1, 2)]
        levels.append([(left[p], left[p - 1] if p else None, left[p + 1]) for p in gone])
        left = [cell for pos, cell in enumerate(left) if pos not in gone]
    return levels


def reduce_lines(load, count):
    sub = lax.broadcasted_iota(jnp.int32, (8, LANE), 0)
    first, last = sub == 0, sub == 7
    one, zero = jnp.full((8, LANE), 1.0, F32), jnp.zeros((8, LANE), F32)
    d0, d1, r0, r1 = ([load(t, q) for t in range(count)] for q in range(4))
    on0 = [d >= 0.0 for d in d0]
    on1 = [d >= 0.0 for d in d1]
    r0 = [jnp.where(on, r, zero) for on, r in zip(on0, r0)]
    r1 = [jnp.where(on, r, zero) for on, r in zip(on1, r1)]
    flag1 = [jnp.where(on, one, zero) for on in on1]
    before = [jnp.where(first, one, roll(flag1[-1], 1, 0))] + flag1[:-1]
    edge_in = [jnp.where(on, b, zero) for on, b in zip(on0, before)]
    edge_mid = [jnp.where(on, f, zero) for on, f in zip(on0, flag1)]
    edge_out = edge_in[1:] + [jnp.where(last, one, roll(edge_in[0], -1, 0))]
    leak0 = [jnp.where(on, d + (2.0 - a - b), one) for on, d, a, b in zip(on0, d0, edge_in, edge_mid)]
    leak1 = [jnp.where(on, d + (2.0 - a - b), one) for on, d, a, b in zip(on1, d1, edge_mid, edge_out)]
    out_leak = jnp.where(last, roll(jnp.where(on0[0], zero, one), -1, 0), zero)
    out_src = zero
    inv0 = [1.0 / (d + (a + b)) for d, a, b in zip(leak0, edge_in, edge_mid)]
    part_leak = [d * i for d, i in zip(leak0, inv0)]
    part_src = [r * i for r, i in zip(r0, inv0)]
    give_leak = [e * p for e, p in zip(edge_in, part_leak)]
    give_src = [e * p for e, p in zip(edge_in, part_src)]
    low_leak, low_src = roll(give_leak[0], -1, 0), roll(give_src[0], -1, 0)
    out_leak, out_src = out_leak + low_leak, out_src + low_src
    give_leak = give_leak[1:] + [jnp.where(last, zero, low_leak)]
    give_src = give_src[1:] + [jnp.where(last, zero, low_src)]
    leak = [d + (e * p + g) for d, e, p, g in zip(leak1, edge_mid, part_leak, give_leak)]
    src = [r + (e * p + g) for r, e, p, g in zip(r1, edge_mid, part_src, give_src)]
    edge = [a * (b * i) for a, b, i in zip(edge_in, edge_mid, inv0)]
    kept = {}
    for level in eliminate_levels(count):
        updates = []
        for cell, low, high in level:
            lo_edge, hi_edge = edge[cell], edge[high]
            inv = 1.0 / (leak[cell] + (lo_edge + hi_edge))
            lo_share, hi_share = lo_edge * inv, hi_edge * inv
            kept[cell] = (lo_share, hi_share, src[cell] * inv)
            updates.append((cell, low, high, lo_edge * hi_share, lo_share, hi_share))
        for cell, low, high, joined, lo_share, hi_share in updates:
            low_leak, low_src = lo_share * leak[cell], lo_share * src[cell]
            if low is None:
                low_leak, low_src = roll(low_leak, -1, 0), roll(low_src, -1, 0)
                out_leak, out_src = out_leak + low_leak, out_src + low_src
                low, low_leak, low_src = count - 1, jnp.where(last, zero, low_leak), jnp.where(last, zero, low_src)
            leak[low], src[low] = leak[low] + low_leak, src[low] + low_src
            leak[high], src[high] = leak[high] + hi_share * leak[cell], src[high] + hi_share * src[cell]
            edge[high] = joined
    end_leak, end_src, lo_edge = leak[-1], src[-1], edge[-1]
    hi_edge = jnp.where(last, zero, roll(lo_edge, -1, 0))
    hops = []
    for hop in (1, 2, 4):
        gone = lax.rem(sub, 2 * hop) == hop - 1
        inv = 1.0 / jnp.where(gone, end_leak + (lo_edge + hi_edge), one)
        lo_share = jnp.where(gone, lo_edge * inv, zero)
        hi_share = jnp.where(gone, hi_edge * inv, zero)
        hops.append((hop, gone, lo_share, hi_share, end_src * inv))
        low_leak, low_src = roll(lo_share * end_leak, -hop, 0), roll(lo_share * end_src, -hop, 0)
        out_leak, out_src = out_leak + low_leak, out_src + low_src
        joined = lo_edge * hi_share
        end_leak, end_src = (
            end_leak + (jnp.where(last, zero, low_leak) + roll(hi_share * end_leak, hop, 0)),
            end_src + (jnp.where(last, zero, low_src) + roll(hi_share * end_src, hop, 0)),
        )
        lo_edge, hi_edge = roll(joined, hop, 0), jnp.where(last, zero, roll(joined, -hop, 0))
    end_leak = jnp.where(on1[-1], end_leak, -one)

    def back(own, previous):
        ends = jnp.where(last, own, zero)
        for hop, gone, lo_share, hi_share, value in reversed(hops):
            lower = jnp.where(sub < hop, previous, roll(ends, hop, 0))
            ends = jnp.where(gone, value + (lo_share * lower + hi_share * roll(ends, -hop, 0)), ends)
        value = [None] * count
        value[-1] = ends
        wrapped = jnp.where(first, previous, roll(ends, 1, 0))
        for level in reversed(eliminate_levels(count)):
            for cell, low, high in level:
                lo_share, hi_share, part = kept[cell]
                lower = wrapped if low is None else value[low]
                value[cell] = part + (lo_share * lower + hi_share * value[high])
        pairs = []
        for t in range(count):
            lower = wrapped if t == 0 else value[t - 1]
            pairs.append((part_src[t] + (edge_in[t] * lower + edge_mid[t] * value[t]) * inv0[t], value[t]))
        return pairs

    return (end_leak, end_src, lo_edge, out_leak, out_src), back


def solve_ends(groups):
    count = len(groups)
    on = [g[0] >= 0.0 for g in groups]
    edges = [jnp.zeros_like(groups[0][0])]
    for i in range(1, count):
        edges.append(jnp.where(jnp.logical_and(on[i - 1], on[i]), groups[i][2], 0.0))
    leaks, srcs = [], []
    for i in range(count):
        leak, src, lo_edge = groups[i][:3]
        leak = leak + (lo_edge - edges[i])
        if i + 1 < count:
            leak = leak + (groups[i + 1][3] + (groups[i + 1][2] - edges[i + 1]))
            src = src + groups[i + 1][4]
        else:
            leak = leak + 1.0
        leaks.append(jnp.where(on[i], leak, 1.0))
        srcs.append(jnp.where(on[i], src, 0.0))
    inverse = []
    for i in range(count):
        if i + 1 < count:
            inv = 1.0 / (leaks[i] + edges[i + 1])
            share = edges[i + 1] * inv
            leaks[i + 1] = leaks[i + 1] + share * leaks[i]
            srcs[i + 1] = srcs[i + 1] + share * srcs[i]
        else:
            inv = 1.0 / leaks[i]
        inverse.append(inv)
    values = [None] * count
    values[-1] = srcs[-1] * inverse[-1]
    for i in reversed(range(count - 1)):
        values[i] = (srcs[i] + edges[i + 1] * values[i + 1]) * inverse[i]
    return values


def far_first(i, count):
    side = 1 - 2 * lax.rem(i, 2)
    return count // 2 + side * lax.div(i + 1, 2)


def sweep_kernel(
    count_x, count_y, basins,
    sol_hbm, forc_hbm, visc_hbm, blk_hbm, layers_hbm, frozen_hbm, basin_hbm,
    smooth_ref, column_ref, total_ref,
    sol_ref, forc_ref, visc_ref, blk_ref, layers_ref, frozen_ref, basin_ref,
    edge_out, edge_in, side_out, side_in, halo_out, halo_in, row_out, row_in, line_out, line_in, ends_buf,
    core_out, core_in, ring_buf, plane_buf, load_sem, send_sem, recv_sem, ready_sem,
):
    cx, cz = factors(count_x)
    rows, lanes = visc_ref.shape
    y_cells = layers_ref.shape[1]
    layers = lanes // y_cells
    chunks = lanes // LANE
    group = 2 * cz
    seg = group // 8
    gx, gy = lax.axis_index("gx"), lax.axis_index("gy")
    core = lax.rem(gx, 2)
    pz = lax.rem(lax.div(gx, 2), cz)
    px = lax.div(gx, 2 * cz)
    partner = gx + 1 - 2 * core
    skip = min(SKIP, group - chunks)
    place = 2 * pz + core - skip
    owning = jnp.logical_and(place >= 0, place < chunks)
    low_edge = jnp.logical_and(owning, place == 0)
    high_edge = jnp.logical_and(owning, place == 1)
    order = [0, chunks - 1] + list(range(1, chunks - 1))
    place_of = {chunk: i for i, chunk in enumerate(order)}
    member = 2 * pz + core

    def along_y(step):
        return lax.rem(gy + step + count_y, count_y)

    def gx_of(x, z, c):
        return (x * cz + z) * 2 + c

    def owner_of(place):
        return gx_of(px, lax.div(place + skip, 2), lax.rem(place + skip, 2))

    loads = [
        pltpu.make_async_copy(src, dst, load_sem.at[i])
        for i, (src, dst) in enumerate((
            (layers_hbm, layers_ref), (frozen_hbm, frozen_ref), (sol_hbm, sol_ref),
            (visc_hbm, visc_ref), (blk_hbm, blk_ref), (forc_hbm, forc_ref), (basin_hbm, basin_ref),
        ))
    ]
    for copy in loads:
        copy.start()

    barrier = pltpu.get_barrier_semaphore()

    def greet(y):
        def one(i, carry):
            to = gx_of(px, cz - 1 - lax.div(i, 2), lax.rem(i, 2))

            @pl.when(jnp.logical_or(to != gx, y != gy))
            def _():
                pl.semaphore_signal(barrier, inc=1, device_id=(to, y), device_id_type=MESH)

            return carry

        return one

    @pl.when(owning)
    def _():
        lax.fori_loop(0, group, greet(gy), 0)
        for i in range(1, cx):
            pl.semaphore_signal(
                barrier, inc=1, device_id=(gx_of(lax.rem(px + i, cx), pz, core), gy),
                device_id_type=MESH,
            )

    @pl.when(low_edge)
    def _():
        lax.fori_loop(0, group, greet(along_y(-1)), 0)

    @pl.when(high_edge)
    def _():
        lax.fori_loop(0, group, greet(along_y(1)), 0)

    def remote(src, dst, k, to):
        return pltpu.make_async_remote_copy(
            src_ref=src, dst_ref=dst, send_sem=send_sem.at[k], recv_sem=recv_sem.at[k],
            device_id=to, device_id_type=MESH,
        )

    def wait_rows(sem, ref, count):
        view = ref.at[pl.ds(0, count)]
        pltpu.make_async_copy(view, view, sem).wait()

    for step in (1, -1):
        pl.semaphore_signal(barrier, inc=1, device_id=(gx, along_y(step)), device_id_type=MESH)

    lane = lax.broadcasted_iota(jnp.int32, (rows, lanes), 1)

    def cell_of(index):
        return ((index.astype(F32) + 0.5) * (1.0 / layers)).astype(jnp.int32)

    layer = lane - cell_of(lane) * layers
    wide = lax.broadcasted_iota(jnp.int32, (y_cells, lanes), 1)
    spread = jnp.where(
        cell_of(wide) == lax.broadcasted_iota(jnp.int32, (y_cells, lanes), 0), 1.0, 0.0
    ).astype(F32)
    loads[0].wait()
    loads[1].wait()
    filled = jnp.dot(layers_ref[...].astype(F32), spread, precision=HIGHEST, preferred_element_type=F32)
    frozen = jnp.dot(frozen_ref[...].astype(F32), spread, precision=HIGHEST, preferred_element_type=F32)
    active = layer.astype(F32) + 0.5 < filled
    bottom, top = layer == 0, layer == layers - 1
    slide = 1.0 - frozen

    def masked(value):
        return jnp.where(active, value, 0.0)

    loads[2].wait()
    state = [masked(sol_ref[k]) for k in range(4)]
    small = lax.broadcasted_iota(jnp.int32, (rows, LANE), 1)

    def facing_up(value):
        return jnp.where(small < layers, roll(value[:, lanes - LANE:], layers), 0.0)

    def facing_down(value):
        return jnp.where(small >= LANE - layers, roll(value[:, :LANE], LANE - layers), 0.0)

    def inner_neighbours(values):
        out = []
        for v in values:
            before = jnp.where(lane < layers, 0.0, roll(v, layers))
            after = jnp.where(lane >= lanes - layers, 0.0, roll(v, lanes - layers))
            below = jnp.where(bottom, v * slide, roll(v, 1))
            above = jnp.where(top, 0.0, roll(v, lanes - 1))
            out.append((before + after) + (below + above))
        return out

    def block(k, j):
        return blk_ref[4 * k + j]

    for k in range(3):
        edge_out[0, pl.ds(k * rows, rows)] = facing_up(state[k])
        edge_out[1, pl.ds(k * rows, rows)] = facing_down(state[k])
    around = inner_neighbours(state[:3])
    wide_rows = 2 * rows
    loads[6].wait()
    names = basin_ref[...].astype(F32)
    for side, column in ((0, y_cells - 1), (1, 0)):
        side_out[side, pl.ds(rows, rows)] = jnp.broadcast_to(names[:, column:column + 1], (rows, LANE))
    loads[3].wait()
    weight = masked(0.25 * visc_ref[...])
    side_out[0, pl.ds(0, rows)] = facing_up(weight)
    side_out[1, pl.ds(0, rows)] = facing_down(weight)
    loads[4].wait()
    loads[5].wait()
    inv_visc = 1.0 / visc_ref[...]
    for k in range(3):
        acc = forc_ref[k]
        for j in range(4):
            if j != k:
                acc = acc - block(k, j) * state[j]
        rhs = masked(acc * inv_visc + 0.25 * around[k])
        diag = jnp.where(active, block(k, k) * inv_visc, -1.0)
        for j in range(chunks):
            at = place_of[j] * 16 + k * wide_rows
            row_out[pl.ds(at, rows)] = diag[:, j * LANE:(j + 1) * LANE]
            row_out[pl.ds(at + rows, rows)] = rhs[:, j * LANE:(j + 1) * LANE]

    @pl.when(owning)
    def _():
        pl.semaphore_wait(barrier, chunks - 1 + 4 + cx - 1)

    @pl.when(jnp.logical_not(owning))
    def _():
        pl.semaphore_wait(barrier, chunks + 4)

    def to_owner(i, carry):
        at = chunks - 1 - i
        to = owner_of(at)
        src = row_out.at[pl.ds(pl.multiple_of(at * 16, 16), 3 * wide_rows)]
        dst = row_in.at[pl.ds(pl.multiple_of(member * 16, 16), 3 * wide_rows)]

        @pl.when(to == gx)
        def _():
            pltpu.make_async_copy(src, dst, recv_sem.at[4]).start()

        @pl.when(to != gx)
        def _():
            remote(src, dst, 4, (to, gy)).start()

        return carry

    for side, step in ((0, 1), (1, -1)):
        remote(
            edge_out.at[side],
            edge_in.at[side, pl.ds(pl.multiple_of(member * 8, 8), 8)],
            side, (owner_of(side), along_y(step)),
        ).start()
    lax.fori_loop(0, chunks, to_owner, 0)

    sides = []
    for side, step in ((0, 1), (1, -1)):
        copy = remote(side_out.at[side], side_in.at[side], 11 + side, (gx, along_y(step)))
        copy.start()
        sides.append(copy)

    @pl.when(owning)
    def _():
        @pl.when(low_edge)
        def _():
            wait_rows(recv_sem.at[0], edge_in.at[0], group * 8)

        @pl.when(high_edge)
        def _():
            wait_rows(recv_sem.at[1], edge_in.at[1], group * 8)

        wait_rows(recv_sem.at[4], row_in, group * 3 * wide_rows)
        low_on = jnp.logical_and(low_edge, gy > 0)
        high_on = jnp.logical_and(high_edge, gy < count_y - 1)
        ways = []
        for k in range(3):
            def load(t, q, k=k):
                value = row_in[pl.ds(t * 16 + k * wide_rows + q, 8, stride=seg * 16), :]
                if q >= rows:
                    at = pl.ds(t * 8 + k * rows + q - rows, 8, stride=seg * 8)
                    low = jnp.where(low_on, edge_in[0, at, :], 0.0)
                    high = jnp.where(high_on, edge_in[1, at, :], 0.0)
                    value = value + 0.25 * (low + high)
                return value

            found, back = reduce_lines(load, seg)
            for i, value in enumerate(found):
                ends_buf[px, 3 * i + k:3 * i + k + 1] = value[7:8]
            ways.append(back)

        for i in range(cx - 1):
            x = lax.rem(px + far_first(i, cx), cx)
            remote(ends_buf.at[px], ends_buf.at[px], 10, (gx_of(x, pz, core), gy)).start()
        wait_rows(recv_sem.at[10], ends_buf, cx - 1)
        ends = solve_ends([[ends_buf[x, 3 * i:3 * i + 3] for i in range(5)] for x in range(cx)])
        own, previous = jnp.zeros((3, LANE), F32), jnp.zeros((3, LANE), F32)
        for x in range(cx):
            own = jnp.where(px == x, ends[x], own)
            previous = jnp.where(px == x + 1, ends[x], previous)
        for k in range(3):
            for t, pair in enumerate(ways[k](own[k:k + 1], previous[k:k + 1])):
                for r in range(rows):
                    line_out[pl.ds(t * 8 + k * rows + r, 8, stride=seg * 8), :] = pair[r]

        def give(i, carry):
            z = lax.rem(pz + far_first(lax.div(i, 2), cz), cz)
            m = 2 * z + lax.rem(i, 2)
            to = gx_of(px, z, lax.rem(i, 2))
            src = line_out.at[pl.ds(pl.multiple_of(m * 8, 8), 3 * rows)]
            dst = line_in.at[pl.ds(pl.multiple_of(place * 8, 8), 3 * rows)]

            @pl.when(to == gx)
            def _():
                pltpu.make_async_copy(src, dst, recv_sem.at[5]).start()

            @pl.when(to != gx)
            def _():
                remote(src, dst, 5, (to, gy)).start()

            return carry

        lax.fori_loop(0, group, give, 0)

    eye = lax.broadcasted_iota(jnp.int32, (y_cells, y_cells), 0) == lax.broadcasted_iota(
        jnp.int32, (y_cells, y_cells), 1
    )
    basin_idx = lax.broadcasted_iota(jnp.int32, (y_cells, basins), 1).astype(F32)
    belongs = []
    for x in range(rows):
        column = jnp.sum(jnp.where(eye, names[x:x + 1], 0.0), axis=1, keepdims=True)
        belongs.append(jnp.where(basin_idx == column, 1.0, 0.0).astype(F32))

    for copy in sides:
        copy.wait_recv()
    wait_rows(recv_sem.at[5], line_in, chunks * 3 * rows)
    solved = [
        jnp.concatenate([line_in[pl.ds(place_of[j] * 8 + k * rows, rows)] for j in range(chunks)], 1)
        for k in range(3)
    ]
    change = [solved[k] - state[k] for k in range(3)]

    beside = []
    for side, on in ((0, gy > 0), (1, gy < count_y - 1)):
        given = jnp.where(on, side_in[side, pl.ds(0, rows)], 0.0)
        at = (lanes - LANE) * side
        beside.append([
            jnp.sum(given * change[k][:, at:at + LANE], axis=1, keepdims=True) for k in range(3)
        ])
    halos = []
    for side, step in ((0, 1), (1, -1)):
        for k in range(3):
            halo_out[side, pl.ds(k * rows, rows)] = jnp.broadcast_to(beside[1 - side][k], (rows, LANE))
        copy = remote(halo_out.at[side], halo_in.at[side], 2 + side, (gx, along_y(step)))
        copy.start()
        halos.append(copy)

    reach = 1
    rounds = []
    while reach < count_y // 2:
        rounds.append(reach)
        reach *= 2

    def tell(k):
        for step in (rounds[k], -rounds[k]):
            pl.semaphore_signal(
                ready_sem.at[k], inc=1, device_id=(gx, along_y(step)), device_id_type=MESH
            )

    if rounds:
        tell(0)
    acc = forc_ref[3] - block(3, 3) * state[3]
    for k in range(3):
        acc = acc - block(3, k) * solved[k]
    step = masked(acc * inv_visc)
    for k in range(3):
        smooth_ref[k] = jnp.where(active, solved[k], sol_ref[k])
    smooth_ref[3] = sol_ref[3] + step
    around = inner_neighbours(change)
    coupled = []
    for k in range(3):
        acc = block(k, 3) * step
        for j in range(3):
            if j != k:
                acc = acc + block(k, j) * change[j]
        coupled.append(acc)
    post = [masked(0.25 * visc_ref[...] * around[k] - coupled[k]) for k in range(3)]
    post.append((visc_ref[...] - block(3, 3)) * step)
    by_row = jnp.concatenate([post[k][x:x + 1] for x in range(rows) for k in range(4)], 0)
    sums = lax.dot_general(
        by_row, spread, (((1,), (1,)), ((), ())), precision=HIGHEST, preferred_element_type=F32
    )
    part = jnp.dot(sums[0:4], belongs[0], precision=HIGHEST, preferred_element_type=F32)
    for x in range(1, rows):
        part = part + jnp.dot(
            sums[4 * x:4 * x + 4], belongs[x], precision=HIGHEST, preferred_element_type=F32
        )

    index4 = lax.broadcasted_iota(jnp.int32, (4, basins), 1).astype(F32)
    for side in range(2):
        for x in range(rows):
            amount = jnp.concatenate(
                [beside[side][k][x:x + 1] for k in range(3)] + [jnp.zeros((1, 1), F32)], 0
            )
            name = side_in[side, rows + x:rows + x + 1, 0:1]
            part = part + jnp.where(index4 == name, amount, 0.0)

    pieces = basins // LANE

    def packed(pair):
        return jnp.concatenate([pair[:, j * LANE:(j + 1) * LANE] for j in range(pieces)], 0)

    lower, upper = packed(part[0:2]), packed(part[2:4])
    core_out[0] = jnp.where(core == 0, upper, lower)
    first = remote(core_out.at[0], core_in.at[0], 6, (partner, gy))
    first.start()
    if rounds:
        pl.semaphore_wait(ready_sem.at[0], 2)
        for k in range(1, len(rounds)):
            tell(k)
            if k + 1 < len(rounds):
                pl.semaphore_wait(ready_sem.at[k], 2)
    first.wait_recv()
    own = jnp.where(core == 0, lower, upper) + core_in[0]
    ring_buf[pz] = own

    def to_ring(i, carry):
        z = lax.rem(pz + far_first(i, cz), cz)
        remote(ring_buf.at[pz], ring_buf.at[pz], 7, (gx_of(px, z, core), gy)).start()
        return carry

    lax.fori_loop(0, cz - 1, to_ring, 0)
    for copy in halos:
        copy.wait_recv()
    column_idx = lax.broadcasted_iota(jnp.int32, (1, y_cells), 1)
    for x in range(rows):
        for k in range(4):
            value = sums[4 * x + k:4 * x + k + 1]
            if k < 3:
                at = k * rows + x
                low, high = (halo_in[side, at:at + 1, 0:y_cells] for side in range(2))
                value = value + jnp.where(column_idx == 0, low, 0.0)
                value = value + jnp.where(column_idx == y_cells - 1, high, 0.0)
            column_ref[k, x:x + 1, :] = value
    wait_rows(recv_sem.at[7], ring_buf, cz - 1)
    own = ring_buf[0]
    for i in range(1, cz):
        own = own + ring_buf[i]
    if len(rounds) > 1:
        pl.semaphore_wait(ready_sem.at[len(rounds) - 1], 2)
    here = px * count_y + gy
    plane_buf[here] = own

    def to_plane(i, carry):
        x = lax.rem(px + far_first(lax.rem(i, cx), cx), cx)
        y = lax.rem(gy + far_first(lax.div(i, cx), count_y), count_y)
        remote(plane_buf.at[here], plane_buf.at[here], 8, (gx_of(x, pz, core), y)).start()
        return carry

    lax.fori_loop(0, cx * count_y - 1, to_plane, 0)
    wait_rows(recv_sem.at[8], plane_buf, cx * count_y - 1)
    own = plane_buf[0]
    for i in range(1, cx * count_y):
        own = own + plane_buf[i]
    core_out[1] = own
    last = remote(core_out.at[1], core_in.at[1], 9, (partner, gy))
    last.start()
    last.wait_recv()
    other = core_in[1]
    lower, upper = jnp.where(core == 0, own, other), jnp.where(core == 0, other, own)
    for j in range(pieces):
        width = min(LANE, total_ref.shape[1] - j * LANE)
        if width > 0:
            total_ref[0:2, j * LANE:j * LANE + width] = lower[2 * j:2 * j + 2, :width]
            total_ref[2:4, j * LANE:j * LANE + width] = upper[2 * j:2 * j + 2, :width]

    for copy in sides + halos + [first, last]:
        copy.wait_send()
    for side in range(2):
        wait_rows(send_sem.at[side], edge_out.at[side], 8)

    @pl.when(owning)
    def _():
        wait_rows(send_sem.at[4], row_out, (chunks - 1) * 3 * wide_rows)
        wait_rows(send_sem.at[5], line_out, (group - 1) * 3 * rows)
        wait_rows(send_sem.at[10], ends_buf, cx - 1)

    @pl.when(jnp.logical_not(owning))
    def _():
        wait_rows(send_sem.at[4], row_out, chunks * 3 * wide_rows)

    wait_rows(send_sem.at[7], ring_buf, cz - 1)
    wait_rows(send_sem.at[8], plane_buf, cx * count_y - 1)


def solution(mesh):
    count_x, count_y = mesh.shape["gx"], mesh.shape["gy"]
    cx, cz = factors(count_x)

    def local(sol, forc, visc, blocks, layers, frozen, basin_map):
        rows, lanes = visc.shape
        chunks = lanes // LANE
        basins = count_x // 2 * count_y
        padded = -(-basins // LANE) * LANE
        size = 2 * padded // LANE
        vmem = pl.BlockSpec(memory_space=pltpu.VMEM)
        anywhere = pl.BlockSpec(memory_space=pl.ANY)
        results = (
            jax.ShapeDtypeStruct(sol.shape, F32),
            jax.ShapeDtypeStruct((4,) + layers.shape, F32),
            jax.ShapeDtypeStruct((4, basins), F32),
        )
        inputs = (sol, forc, visc, blocks, layers, frozen, basin_map)
        return pl.pallas_call(
            functools.partial(sweep_kernel, count_x, count_y, padded),
            out_shape=results,
            in_specs=[anywhere] * 7,
            out_specs=(vmem, vmem, vmem),
            scratch_shapes=[pltpu.VMEM(a.shape, a.dtype) for a in inputs] + [
                pltpu.VMEM((2, 8, LANE), F32),
                pltpu.VMEM((2, 2 * cz * 8, LANE), F32),
                pltpu.VMEM((2, 2 * rows, LANE), F32),
                pltpu.VMEM((2, 2 * rows, LANE), F32),
                pltpu.VMEM((2, 3 * rows, LANE), F32),
                pltpu.VMEM((2, 3 * rows, LANE), F32),
                pltpu.VMEM((chunks * 16, LANE), F32),
                pltpu.VMEM((2 * cz * 16, LANE), F32),
                pltpu.VMEM((2 * cz * 8, LANE), F32),
                pltpu.VMEM((chunks * 8, LANE), F32),
                pltpu.VMEM((cx, 16, LANE), F32),
                pltpu.VMEM((2, size, LANE), F32),
                pltpu.VMEM((2, size, LANE), F32),
                pltpu.VMEM((cz, size, LANE), F32),
                pltpu.VMEM((cx * count_y, size, LANE), F32),
                pltpu.SemaphoreType.DMA((7,)),
                pltpu.SemaphoreType.DMA((13,)),
                pltpu.SemaphoreType.DMA((13,)),
                pltpu.SemaphoreType.REGULAR((4,)),
            ],
            compiler_params=pltpu.CompilerParams(
                collective_id=0, has_side_effects=True, vmem_limit_bytes=63 * 2**20
            ),
            name="sweep",
        )(*inputs)
    return jax.shard_map(
        local,
        mesh=mesh,
        in_specs=(
            P(None, "gx", "gy"), P(None, "gx", "gy"), P("gx", "gy"), P(None, "gx", "gy"),
            P("gx", "gy"), P("gx", "gy"), P("gx", "gy"),
        ),
        out_specs=(P(None, "gx", "gy"), P(None, "gx", "gy"), P()),
        check_vma=False,
    )
```

time: 59.5 us -> 53.7 us (0.903)
  Pallas kernels: 55.9 us -> 50.2 us
    pallas_call x1, Pallas kernels: 55.9 us -> 50.2 us  [local(): pl.pallas_call(functools.partial(sweep_kernel, count_x, count_y, padded),...]
where the time goes in v2:
time: 53.7 us; the launch traced here: 53.5 us
  Pallas kernels  50.2 us (93%)
  local copies, waits for them, and re-layouts  2.69 us (5%)
  between operations  0.65 us (1%)
    pallas_call x1, Pallas kernels, local(): pl.pallas_call(functools.partial(sweep_kernel, count_x, count_y, padded),...  50.2 us
    unnamed x7, local copies, waits for them, and re-layouts  2.69 us

profile of v2, /device:TPU:1, one launch (start us, length us, event | category | flops | bytes accessed | tf_op | source)
XLA Modules:
  0.0 53.5 jit_solution(8927734150695657424)
XLA Ops:
  0.6 50.2 %sweep.1 = (f32[4,2,1280]{2,1,0:T(2,128)}, f32[4,2,16]{2,1,0:T(2,128)}, f32[4,384]{1,0:T(4,128)}) custom-call(f32[4,2,1280]{2,1,0:T(2,128)} %sol_hbm.1, f32[4,2,1280]{2,1,0:T(2,128)} %forc_hbm.1, f32[2,1280]{1,0:T(2,128)} %visc_hbm.1, f32[16,2,1280]{2,1,0:T(2,128)} %blk_hbm.1, s32[2,16]{1,0:T(2,128)} %layers_hbm.1, s32[2,16]{1,0:T(2,128)} %frozen_hbm.1, ...), custom_call_target="tpu_custom_call" | custom-call | tf_op jit(solution)/shard_map/sweep/pallas_call | solution.py:617
  50.8 0.0 copy-start.1
  50.8 1.4 %copy.13 = f32[4,2,1280]{2,1,0:T(2,128)} copy(f32[4,2,1280]{2,1,0:T(2,128)} %get-tuple-element.6) | data formatting | bytes 81920
  52.2 0.0 copy-done.1
  52.2 0.0 copy-start
  52.2 0.6 %copy.14 = f32[4,2,16]{2,1,0:T(2,128)} copy(f32[4,2,16]{2,1,0:T(2,128)S(1)} %copy-done.1) | data formatting | bytes 1024
  52.8 0.1 copy-done
  52.9 0.6 %copy.15 = f32[4,384]{1,0:T(4,128)} copy(f32[4,384]{1,0:T(4,128)S(1)} %copy-done) | data formatting | bytes 12288
Async XLA Ops:
  50.8 1.4 %copy-start.1 = (f32[4,2,16]{2,1,0:T(2,128)S(1)}, f32[4,2,16]{2,1,0:T(2,128)}, u32[]{:S(2)}) copy-start(f32[4,2,16]{2,1,0:T(2,128)} %get-tuple-element.7) | copy-start | bytes 1540
  52.2 0.7 %copy-start = (f32[4,384]{1,0:T(4,128)S(1)}, f32[4,384]{1,0:T(4,128)}, u32[]{:S(2)}) copy-start(f32[4,384]{1,0:T(4,128)} %get-tuple-element.8) | copy-start | bytes 18436

commit v3 on v2

--- a/solution.py
+++ b/solution.py
@@ -11,7 +11,7 @@
 HIGHEST = lax.Precision.HIGHEST
 F32 = jnp.float32
 LANE = 128
-SKIP = 3
+SEATS = (1, 2, 3, 5, 6, 8, 10, 11, 13, 15)
 
 
 def factors(count_x):
@@ -181,14 +181,16 @@
     pz = lax.rem(lax.div(gx, 2), cz)
     px = lax.div(gx, 2 * cz)
     partner = gx + 1 - 2 * core
-    skip = min(SKIP, group - chunks)
-    place = 2 * pz + core - skip
-    owning = jnp.logical_and(place >= 0, place < chunks)
+    seats = SEATS if group >= 24 else tuple(range(1, chunks + 1))
+    member = 2 * pz + core
+    place = jnp.int32(chunks)
+    for i in range(chunks):
+        place = jnp.where(member == seats[i], i, place)
+    owning = place < chunks
     low_edge = jnp.logical_and(owning, place == 0)
     high_edge = jnp.logical_and(owning, place == 1)
     order = [0, chunks - 1] + list(range(1, chunks - 1))
     place_of = {chunk: i for i, chunk in enumerate(order)}
-    member = 2 * pz + core
 
     def along_y(step):
         return lax.rem(gy + step + count_y, count_y)
@@ -197,7 +199,7 @@
         return (x * cz + z) * 2 + c
 
     def owner_of(place):
-        return gx_of(px, lax.div(place + skip, 2), lax.rem(place + skip, 2))
+        return gx_of(px, seats[place] // 2, seats[place] % 2)
 
     loads = [
         pltpu.make_async_copy(src, dst, load_sem.at[i])
@@ -333,21 +335,17 @@
     def _():
         pl.semaphore_wait(barrier, chunks + 4)
 
-    def to_owner(i, carry):
-        at = chunks - 1 - i
-        to = owner_of(at)
-        src = row_out.at[pl.ds(pl.multiple_of(at * 16, 16), 3 * wide_rows)]
+    def to_owner(at):
+        src = row_out.at[pl.ds(at * 16, 3 * wide_rows)]
         dst = row_in.at[pl.ds(pl.multiple_of(member * 16, 16), 3 * wide_rows)]
 
-        @pl.when(to == gx)
+        @pl.when(place == at)
         def _():
             pltpu.make_async_copy(src, dst, recv_sem.at[4]).start()
 
-        @pl.when(to != gx)
+        @pl.when(place != at)
         def _():
-            remote(src, dst, 4, (to, gy)).start()
-
-        return carry
+            remote(src, dst, 4, (owner_of(at), gy)).start()
 
     for side, step in ((0, 1), (1, -1)):
         remote(
@@ -355,7 +353,8 @@
             edge_in.at[side, pl.ds(pl.multiple_of(member * 8, 8), 8)],
             side, (owner_of(side), along_y(step)),
         ).start()
-    lax.fori_loop(0, chunks, to_owner, 0)
+    for at in reversed(range(chunks)):
+        to_owner(at)
 
     sides = []
     for side, step in ((0, 1), (1, -1)):
@@ -509,30 +508,20 @@
             part = part + jnp.where(index4 == name, amount, 0.0)
 
     pieces = basins // LANE
-
-    def packed(pair):
-        return jnp.concatenate([pair[:, j * LANE:(j + 1) * LANE] for j in range(pieces)], 0)
-
-    lower, upper = packed(part[0:2]), packed(part[2:4])
-    core_out[0] = jnp.where(core == 0, upper, lower)
-    first = remote(core_out.at[0], core_in.at[0], 6, (partner, gy))
-    first.start()
+    ring_buf[pz] = jnp.concatenate([part[:, j * LANE:(j + 1) * LANE] for j in range(pieces)], 0)
+
+    def to_ring(i, carry):
+        z = lax.rem(pz + far_first(i, cz), cz)
+        remote(ring_buf.at[pz], ring_buf.at[pz], 7, (gx_of(px, z, core), gy)).start()
+        return carry
+
+    lax.fori_loop(0, cz - 1, to_ring, 0)
     if rounds:
         pl.semaphore_wait(ready_sem.at[0], 2)
         for k in range(1, len(rounds)):
             tell(k)
             if k + 1 < len(rounds):
                 pl.semaphore_wait(ready_sem.at[k], 2)
-    first.wait_recv()
-    own = jnp.where(core == 0, lower, upper) + core_in[0]
-    ring_buf[pz] = own
-
-    def to_ring(i, carry):
-        z = lax.rem(pz + far_first(i, cz), cz)
-        remote(ring_buf.at[pz], ring_buf.at[pz], 7, (gx_of(px, z, core), gy)).start()
-        return carry
-
-    lax.fori_loop(0, cz - 1, to_ring, 0)
     for copy in halos:
         copy.wait_recv()
     column_idx = lax.broadcasted_iota(jnp.int32, (1, y_cells), 1)
@@ -565,19 +554,17 @@
     own = plane_buf[0]
     for i in range(1, cx * count_y):
         own = own + plane_buf[i]
-    core_out[1] = own
-    last = remote(core_out.at[1], core_in.at[1], 9, (partner, gy))
+    core_out[...] = own
+    last = remote(core_out, core_in, 9, (partner, gy))
     last.start()
     last.wait_recv()
-    other = core_in[1]
-    lower, upper = jnp.where(core == 0, own, other), jnp.where(core == 0, other, own)
+    own = own + core_in[...]
     for j in range(pieces):
         width = min(LANE, total_ref.shape[1] - j * LANE)
         if width > 0:
-            total_ref[0:2, j * LANE:j * LANE + width] = lower[2 * j:2 * j + 2, :width]
-            total_ref[2:4, j * LANE:j * LANE + width] = upper[2 * j:2 * j + 2, :width]
-
-    for copy in sides + halos + [first, last]:
+            total_ref[:, j * LANE:j * LANE + width] = own[4 * j:4 * j + 4, :width]
+
+    for copy in sides + halos + [last]:
         copy.wait_send()
     for side in range(2):
         wait_rows(send_sem.at[side], edge_out.at[side], 8)
@@ -605,7 +592,7 @@
         chunks = lanes // LANE
         basins = count_x // 2 * count_y
         padded = -(-basins // LANE) * LANE
-        size = 2 * padded // LANE
+        size = 4 * padded // LANE
         vmem = pl.BlockSpec(memory_space=pltpu.VMEM)
         anywhere = pl.BlockSpec(memory_space=pl.ANY)
         results = (
@@ -631,8 +618,8 @@
                 pltpu.VMEM((2 * cz * 8, LANE), F32),
                 pltpu.VMEM((chunks * 8, LANE), F32),
                 pltpu.VMEM((cx, 16, LANE), F32),
-                pltpu.VMEM((2, size, LANE), F32),
-                pltpu.VMEM((2, size, LANE), F32),
+                pltpu.VMEM((size, LANE), F32),
+                pltpu.VMEM((size, LANE), F32),
                 pltpu.VMEM((cz, size, LANE), F32),
                 pltpu.VMEM((cx * count_y, size, LANE), F32),
                 pltpu.SemaphoreType.DMA((7,)),

time: 53.7 us -> 53 us (0.987)
  Pallas kernels: 50.2 us -> 49.4 us
    pallas_call x1, Pallas kernels: 50.2 us -> 49.4 us  [local(): pl.pallas_call(functools.partial(sweep_kernel, count_x, count_y, padded),...]
where the time goes in v3:
time: 53 us; the launch traced here: 52.7 us
  Pallas kernels  49.4 us (93%)
  local copies, waits for them, and re-layouts  2.69 us (5%)
  between operations  0.65 us (1%)
    pallas_call x1, Pallas kernels, local(): pl.pallas_call(functools.partial(sweep_kernel, count_x, count_y, padded),...  49.4 us
    unnamed x7, local copies, waits for them, and re-layouts  2.69 us

profile of v3, /device:TPU:1, one launch (start us, length us, event | category | flops | bytes accessed | tf_op | source)
XLA Modules:
  0.0 52.7 jit_solution(8697927031478962630)
XLA Ops:
  0.6 49.4 %sweep.1 = (f32[4,2,1280]{2,1,0:T(2,128)}, f32[4,2,16]{2,1,0:T(2,128)}, f32[4,384]{1,0:T(4,128)}) custom-call(f32[4,2,1280]{2,1,0:T(2,128)} %sol_hbm.1, f32[4,2,1280]{2,1,0:T(2,128)} %forc_hbm.1, f32[2,1280]{1,0:T(2,128)} %visc_hbm.1, f32[16,2,1280]{2,1,0:T(2,128)} %blk_hbm.1, s32[2,16]{1,0:T(2,128)} %layers_hbm.1, s32[2,16]{1,0:T(2,128)} %frozen_hbm.1, ...), custom_call_target="tpu_custom_call" | custom-call | tf_op jit(solution)/shard_map/sweep/pallas_call | solution.py:604
  50.0 0.0 copy-start.1
  50.0 1.4 %copy.13 = f32[4,2,1280]{2,1,0:T(2,128)} copy(f32[4,2,1280]{2,1,0:T(2,128)} %get-tuple-element.6) | data formatting | bytes 81920
  51.4 0.0 copy-done.1
  51.4 0.0 copy-start
  51.4 0.6 %copy.14 = f32[4,2,16]{2,1,0:T(2,128)} copy(f32[4,2,16]{2,1,0:T(2,128)S(1)} %copy-done.1) | data formatting | bytes 1024
  52.0 0.1 copy-done
  52.1 0.6 %copy.15 = f32[4,384]{1,0:T(4,128)} copy(f32[4,384]{1,0:T(4,128)S(1)} %copy-done) | data formatting | bytes 12288
Async XLA Ops:
  50.0 1.4 %copy-start.1 = (f32[4,2,16]{2,1,0:T(2,128)S(1)}, f32[4,2,16]{2,1,0:T(2,128)}, u32[]{:S(2)}) copy-start(f32[4,2,16]{2,1,0:T(2,128)} %get-tuple-element.7) | copy-start | bytes 1540
  51.4 0.7 %copy-start = (f32[4,384]{1,0:T(4,128)S(1)}, f32[4,384]{1,0:T(4,128)}, u32[]{:S(2)}) copy-start(f32[4,384]{1,0:T(4,128)} %get-tuple-element.8) | copy-start | bytes 18436

commit v4 on v3

--- a/solution.py
+++ b/solution.py
@@ -583,6 +583,18 @@
     wait_rows(send_sem.at[8], plane_buf, cx * count_y - 1)
 
 
+def place_kernel(*refs):
+    half = (len(refs) - 1) // 2
+    copies = [
+        pltpu.make_async_copy(src, dst, refs[-1].at[i])
+        for i, (src, dst) in enumerate(zip(refs[:half], refs[half:-1]))
+    ]
+    for copy in copies:
+        copy.start()
+    for copy in copies:
+        copy.wait()
+
+
 def solution(mesh):
     count_x, count_y = mesh.shape["gx"], mesh.shape["gy"]
     cx, cz = factors(count_x)
@@ -600,8 +612,11 @@
             jax.ShapeDtypeStruct((4,) + layers.shape, F32),
             jax.ShapeDtypeStruct((4, basins), F32),
         )
-        inputs = (sol, forc, visc, blocks, layers, frozen, basin_map)
-        return pl.pallas_call(
+        inputs = tuple(
+            pltpu.with_memory_space_constraint(a, pltpu.HBM)
+            for a in (sol, forc, visc, blocks, layers, frozen, basin_map)
+        )
+        found = pl.pallas_call(
             functools.partial(sweep_kernel, count_x, count_y, padded),
             out_shape=results,
             in_specs=[anywhere] * 7,
@@ -628,10 +643,18 @@
                 pltpu.SemaphoreType.REGULAR((4,)),
             ],
             compiler_params=pltpu.CompilerParams(
-                collective_id=0, has_side_effects=True, vmem_limit_bytes=63 * 2**20
+                collective_id=0, has_side_effects=True, vmem_limit_bytes=32 * 2**20
             ),
             name="sweep",
         )(*inputs)
+        return pl.pallas_call(
+            place_kernel,
+            out_shape=results,
+            in_specs=[pl.BlockSpec(memory_space=pl.ANY)] * 3,
+            out_specs=(pl.BlockSpec(memory_space=pl.ANY),) * 3,
+            scratch_shapes=[pltpu.SemaphoreType.DMA((3,))],
+            name="place",
+        )(*[pltpu.with_memory_space_constraint(a, pltpu.VMEM) for a in found])
     return jax.shard_map(
         local,
         mesh=mesh,

time: 53 us -> 50.2 us (0.947)
  local copies, waits for them, and re-layouts: 2.69 us -> 0 us
    unnamed x7 -> x0, local copies, waits for them, and re-layouts: 2.69 us -> none
    pallas_call x0 -> x1, Pallas kernels: none -> 0.65 us  [local(): pl.pallas_call(place_kernel, out_shape=results, in_specs=[pl.BlockSpec(me...]
    pallas_call x1, Pallas kernels: 49.4 us -> 48.8 us  [local(): pl.pallas_call(functools.partial(sweep_kernel, count_x, count_y, padded),...]
where the time goes in v4:
time: 50.2 us; the launch traced here: 50.1 us
  Pallas kernels  49.4 us (98%)
  between operations  0.64 us (1%)
    pallas_call x1, Pallas kernels, local(): pl.pallas_call(functools.partial(sweep_kernel, count_x, count_y, padded),...  48.8 us

profile of v4, /device:TPU:1, one launch (start us, length us, event | category | flops | bytes accessed | tf_op | source)
XLA Modules:
  0.0 50.1 jit_solution(16943323503395606456)
XLA Ops:
  0.6 48.8 %sweep.1 = (f32[4,2,1280]{2,1,0:T(2,128)S(1)}, f32[4,2,16]{2,1,0:T(2,128)S(1)}, f32[4,384]{1,0:T(4,128)S(1)}) custom-call(f32[4,2,1280]{2,1,0:T(2,128)} %sol_hbm.1, f32[4,2,1280]{2,1,0:T(2,128)} %forc_hbm.1, f32[2,1280]{1,0:T(2,128)} %visc_hbm.1, f32[16,2,1280]{2,1,0:T(2,128)} %blk_hbm.1, s32[2,16]{1,0:T(2,128)} %layers_hbm.1, s32[2,16]{1,0:T(2,128)} %frozen_hbm.1, ...), custom_call_target="tpu_custom_call" | custom-call | tf_op jit(solution)/shard_map/sweep/pallas_call | solution.py:619
  49.4 0.7 %place.1 = (f32[4,2,1280]{2,1,0:T(2,128)}, f32[4,2,16]{2,1,0:T(2,128)}, f32[4,384]{1,0:T(4,128)}) custom-call(f32[4,2,1280]{2,1,0:T(2,128)S(1)} %get-tuple-element.6.refs_0_, f32[4,2,16]{2,1,0:T(2,128)S(1)} %get-tuple-element.7.refs_1_, f32[4,384]{1,0:T(4,128)S(1)} %get-tuple-element.8.refs_2_), custom_call_target="tpu_custom_call" | custom-call | tf_op jit(solution)/shard_map/place/pallas_call | solution.py:650

commit v5 on v4

--- a/solution.py
+++ b/solution.py
@@ -205,11 +205,13 @@
         pltpu.make_async_copy(src, dst, load_sem.at[i])
         for i, (src, dst) in enumerate((
             (layers_hbm, layers_ref), (frozen_hbm, frozen_ref), (sol_hbm, sol_ref),
-            (visc_hbm, visc_ref), (blk_hbm, blk_ref), (forc_hbm, forc_ref), (basin_hbm, basin_ref),
+            (visc_hbm, visc_ref), (blk_hbm.at[pl.ds(0, 12)], blk_ref.at[pl.ds(0, 12)]),
+            (forc_hbm, forc_ref), (basin_hbm, basin_ref),
+            (blk_hbm.at[pl.ds(12, 4)], blk_ref.at[pl.ds(12, 4)]),
         ))
     ]
-    for copy in loads:
-        copy.start()
+    for i in (4, 5, 2, 3, 0, 1, 6, 7):
+        loads[i].start()
 
     barrier = pltpu.get_barrier_semaphore()
 
@@ -424,6 +426,7 @@
 
         lax.fori_loop(0, group, give, 0)
 
+    loads[7].wait()
     eye = lax.broadcasted_iota(jnp.int32, (y_cells, y_cells), 0) == lax.broadcasted_iota(
         jnp.int32, (y_cells, y_cells), 1
     )
@@ -637,7 +640,7 @@
                 pltpu.VMEM((size, LANE), F32),
                 pltpu.VMEM((cz, size, LANE), F32),
                 pltpu.VMEM((cx * count_y, size, LANE), F32),
-                pltpu.SemaphoreType.DMA((7,)),
+                pltpu.SemaphoreType.DMA((8,)),
                 pltpu.SemaphoreType.DMA((13,)),
                 pltpu.SemaphoreType.DMA((13,)),
                 pltpu.SemaphoreType.REGULAR((4,)),

time: 50.2 us -> 50.2 us (level)
  no operation moved by 1% of the time
where the time goes in v5:
time: 50.2 us; the launch traced here: 50.1 us
  Pallas kernels  49.4 us (98%)
  between operations  0.64 us (1%)
    pallas_call x1, Pallas kernels, local(): pl.pallas_call(functools.partial(sweep_kernel, count_x, count_y, padded),...  48.8 us

profile of v5, /device:TPU:1, one launch (start us, length us, event | category | flops | bytes accessed | tf_op | source)
XLA Modules:
  0.0 50.1 jit_solution(80358716343946706)
XLA Ops:
  0.6 48.8 %sweep.1 = (f32[4,2,1280]{2,1,0:T(2,128)S(1)}, f32[4,2,16]{2,1,0:T(2,128)S(1)}, f32[4,384]{1,0:T(4,128)S(1)}) custom-call(f32[4,2,1280]{2,1,0:T(2,128)} %sol_hbm.1, f32[4,2,1280]{2,1,0:T(2,128)} %forc_hbm.1, f32[2,1280]{1,0:T(2,128)} %visc_hbm.1, f32[16,2,1280]{2,1,0:T(2,128)} %blk_hbm.1, s32[2,16]{1,0:T(2,128)} %layers_hbm.1, s32[2,16]{1,0:T(2,128)} %frozen_hbm.1, ...), custom_call_target="tpu_custom_call" | custom-call | tf_op jit(solution)/shard_map/sweep/pallas_call | solution.py:622
  49.4 0.7 %place.1 = (f32[4,2,1280]{2,1,0:T(2,128)}, f32[4,2,16]{2,1,0:T(2,128)}, f32[4,384]{1,0:T(4,128)}) custom-call(f32[4,2,1280]{2,1,0:T(2,128)S(1)} %get-tuple-element.6.refs_0_, f32[4,2,16]{2,1,0:T(2,128)S(1)} %get-tuple-element.7.refs_1_, f32[4,384]{1,0:T(4,128)S(1)} %get-tuple-element.8.refs_2_), custom_call_target="tpu_custom_call" | custom-call | tf_op jit(solution)/shard_map/place/pallas_call | solution.py:653
